TPU v7x, 512 devices: a whole 4x4x16 slice. The times are simulated.
512 devices in a mesh: chan: 128 (over y, z, x_hi), pair: 4 (over x_lo, core).
Axes of the slice: x: 4 (x_hi: 2, x_lo: 2; x = x_hi * 2 + x_lo), y: 4, z: 16, core: 2. Of those that a mesh axis runs over, the one named last changes fastest.
Arguments:
- voltages: bfloat16 [4, 256, 2, 34560], P('pair', 'chan'), may hold values from -6 to 6
- fir_taps: float32 [8, 256], replicated, may hold values from -2 to 2
Outputs:
- visibilities: float32 [128, 2, 1024, 1024], P('chan', None, 'pair')
All inputs are finite; a program needn't handle non-finite values.
Results may differ from a plain program's by a relative error of at most 0.0036.
Values may be sent and summed in bfloat16 or wider, within the bound.
A program may use at most 64 MiB of HBM per device.

v0:
```python
import math

import jax
import jax.numpy as jnp
from jax import lax
from jax.sharding import PartitionSpec as P


def dft_rows(channels):
    frame = 2 * channels
    row_index = jnp.arange(2 * channels, dtype=jnp.int32)
    col_index = jnp.arange(frame, dtype=jnp.int32)
    freq_index = row_index // 2
    phases = freq_index[:, None] * col_index[None, :] % frame
    angles = phases.astype(jnp.float32) * (2.0 * math.pi / frame)
    chosen = jnp.where((row_index % 2 == 0)[:, None], jnp.cos(angles), -jnp.sin(angles))
    return chosen * (1.0 / math.sqrt(frame))


def channelize(sample_rows, fir_taps, transform, spectra_len):
    tap_count, frame = fir_taps.shape
    channels = frame // 2
    framed = sample_rows.astype(jnp.float32).reshape(
        sample_rows.shape[0], spectra_len + tap_count - 1, frame
    )
    filtered = jnp.zeros((sample_rows.shape[0], spectra_len, frame), jnp.float32)
    for tap in range(tap_count):
        filtered = filtered + fir_taps[tap][None, None, :] * framed[:, tap : tap + spectra_len, :]
    spectra = jnp.einsum("wn,asn->aws", transform, filtered, precision=lax.Precision.HIGHEST)
    return spectra.reshape(sample_rows.shape[0], channels, 2 * spectra_len).astype(jnp.bfloat16)


def correlate(own_rows, columns, spectra_len):
    blocks = columns.shape[2] // (2 * spectra_len)
    shaped = columns.reshape(columns.shape[0], columns.shape[1], blocks, 2, spectra_len)
    rotated = jnp.stack([-shaped[:, :, :, 1, :], shaped[:, :, :, 0, :]], axis=3).reshape(
        columns.shape
    )
    stacked = jnp.concatenate([columns, rotated], axis=0)
    stacked = jnp.transpose(stacked, (1, 0, 2))
    own_first = jnp.transpose(own_rows, (1, 0, 2))
    product = jnp.einsum("cik,cjk->cij", own_first, stacked, preferred_element_type=jnp.float32)
    count = columns.shape[0]
    product = product.reshape(product.shape[0], product.shape[1], 2, count)
    return jnp.transpose(product, (0, 2, 1, 3))


def shards(voltages, fir_taps):
    samples = voltages[0]
    batch_count = samples.shape[1]
    tap_count, frame = fir_taps.shape
    spectra_len = samples.shape[2] // frame - tap_count + 1
    transform = dft_rows(frame // 2)
    pieces = [
        channelize(samples[:, batch], fir_taps, transform, spectra_len)
        for batch in range(batch_count)
    ]
    spectra = jnp.concatenate(pieces, axis=2)[None]
    gathered = lax.all_gather(spectra, "pair", axis=0, tiled=True)
    turned = lax.all_to_all(gathered, "chan", split_axis=2, concat_axis=1, tiled=True)
    everyone = turned.reshape(turned.shape[0] * turned.shape[1], turned.shape[2], turned.shape[3])
    own_rows = lax.dynamic_index_in_dim(turned, lax.axis_index("pair"), 0, keepdims=False)
    summed = correlate(own_rows, everyone, spectra_len)
    return summed * (1.0 / math.sqrt(batch_count * spectra_len))


def solution(mesh):
    in_specs = (P("pair", "chan", None, None), P())
    out_specs = P("chan", None, "pair", None)
    return jax.shard_map(shards, mesh=mesh, in_specs=in_specs, out_specs=out_specs, check_vma=False)
```

profile of v0, /device:TPU:1, one launch (start us, length us, event | category | flops | bytes accessed | tf_op | source)
XLA Modules:
  0.0 144.3 jit_solution(16215200199921057058)
XLA Ops:
  6.5 1.0 fusion.70
  7.5 2.8 %fusion.3 = (f32[2,34560]{1,0:T(2,128)S(1)}, f32[2,34560]{1,0:T(2,128)S(1)}) fusion(bf16[2,2,34560]{2,1,0:T(2,128)(2,1)} %bitcast.42), kind=kLoop, calls=%fused_computation.14 | loop fusion | flops 138240 | bytes 829440 | tf_op jit(solution)/shard_map/convert_element_type | solution.py:23
  10.4 0.2 reshape.76
  10.6 1.7 %fusion = bf16[2,256,128]{1,2,0:T(8,128)(2,1)S(1)} fusion(f32[2,135,256]{2,1,0:T(8,128)S(1)} %reshape.76, f32[256]{0:T(256)S(1)} %bitcast.56, f32[256]{0:T(256)S(1)} %bitcast.58, f32[256]{0:T(256)S(1)} %bitcast.46, f32[256]{0:T(256)S(1)} %bitcast.48, f32[256]{0:T(256)S(1)} %bitcast.50, f32[256]{0:T(256)S(1)} %bitcast.52, f32[256]{0:T(256)S(1)} %bitcast.54, ...), kind=kOutput, calls=%fused_computation.4 | convolution fusion | flops 203489280 | bytes 2237952 | tf_op jit(solution)/shard_map/wn,asn->aws/dot_general | solution.py:29
  12.4 0.1 copy.15
  12.6 0.2 reshape.77
  12.8 1.7 %fusion.1 = bf16[2,256,128]{1,2,0:T(8,128)(2,1)S(1)} fusion(f32[2,135,256]{2,1,0:T(8,128)S(1)} %reshape.77, f32[256]{0:T(256)S(1)} %bitcast.57, f32[256]{0:T(256)S(1)} %bitcast.59, f32[256]{0:T(256)S(1)} %bitcast.47, f32[256]{0:T(256)S(1)} %bitcast.49, f32[256]{0:T(256)S(1)} %bitcast.51, f32[256]{0:T(256)S(1)} %bitcast.53, f32[256]{0:T(256)S(1)} %bitcast.55, ...), kind=kOutput, calls=%fused_computation.5 | convolution fusion | flops 203489280 | bytes 2237952 | tf_op jit(solution)/shard_map/wn,asn->aws/dot_general | solution.py:29
  14.5 0.1 copy.16
  14.7 0.7 pad_maximum_fusion.2
  15.5 0.0 all-gather.3.cloned.1.call-update
  15.5 34.2 %all-gather.3.cloned.1.call-done = bf16[8,128,512]{2,1,0:T(8,128)(2,1)} async-done(((bf16[2,128,512]{2,1,0:T(8,128)(2,1)}), bf16[8,128,512]{2,1,0:T(8,128)(2,1)}) %all-gather.3.cloned.1.call-update) | async-done | bytes 1048592 | tf_op jit(solution)/shard_map/all_gather | solution.py:59
  49.7 3.3 %copy.17 = bf16[4,2,128,512]{3,1,0,2:T(2,128)(2,1)} copy(bf16[4,2,128,512]{3,2,1,0:T(8,128)(2,1)} %bitcast.43) | data formatting | bytes 2097152 | tf_op jit(solution)/shard_map/all_gather | solution.py:59
  53.0 18.9 %all-to-all-start = ((bf16[4,2,128,512]{3,1,0,2:T(2,128)(2,1)}), bf16[4,2,128,512]{3,1,0,2:T(2,128)(2,1)S(1)}, u32[]{:S(2)}, u32[]{:S(2)}) async-start(bf16[4,2,128,512]{3,1,0,2:T(2,128)(2,1)} %copy.17), calls=%async_computation | async-start | bytes 2097152 | tf_op jit(solution)/shard_map/all_to_all | solution.py:60
  71.9 53.1 %all-to-all-done = bf16[4,2,128,512]{3,1,0,2:T(2,128)(2,1)S(1)} async-done(((bf16[4,2,128,512]{3,1,0,2:T(2,128)(2,1)}), bf16[4,2,128,512]{3,1,0,2:T(2,128)(2,1)S(1)}, u32[]{:S(2)}, u32[]{:S(2)}) %all-to-all-start) | async-done | bytes 1048608 | tf_op jit(solution)/shard_map/all_to_all | solution.py:60
  124.9 0.7 copy.19
  125.7 1.4 copy.18
  127.1 0.7 reshape_reshape.3
  127.7 0.4 reshape.74
  128.2 2.3 %slice_negate_fusion = (bf16[1024,1,2,1,128]{4,3,2,0,1:T(2,128)(2,1)S(1)}, bf16[1024,1,2,1,128]{4,3,2,0,1:T(2,128)(2,1)S(1)}) fusion(bf16[1024,1,2,2,128]{4,3,2,0,1:T(2,128)(2,1)S(1)} %reshape_reshape.3), kind=kLoop, calls=%fused_computation.6 | loop fusion | flops 262144 | bytes 2097152 | tf_op jit(solution)/shard_map/neg | solution.py:36
  130.6 2.4 %pad_maximum_fusion.1 = bf16[1024,1,2,2,128]{4,3,2,0,1:T(2,128)(2,1)S(1)} fusion(bf16[1024,1,2,1,128]{4,3,2,0,1:T(2,128)(2,1)S(1)} %get-tuple-element.8, bf16[1024,1,2,1,128]{4,3,2,0,1:T(2,128)(2,1)S(1)} %get-tuple-element.7), kind=kLoop, calls=%fused_computation.7 | loop fusion | flops 2097152 | bytes 2097152 | tf_op jit(solution)/shard_map/stack | solution.py:36
  133.0 0.4 reshape.75
  133.4 1.8 %constant_dynamic-slice_fusion = bf16[1,256,1,512]{3,0,1,2:T(2,128)(2,1)S(1)} fusion(bf16[4,256,1,512]{3,0,1,2:T(4,128)(2,1)} %bitcast.41, s32[]{:T(128)S(6)} %select_n.46), kind=kLoop, calls=%fused_computation.81 | loop fusion | bytes 524292 | tf_op jit(solution)/shard_map/jit(dynamic_index_in_dim)/dynamic_slice | solution.py:62
  135.2 0.1 pad_maximum_fusion
  135.4 2.1 %multiply_bitcast_fusion = f32[1,2,256,1024]{3,2,1,0:T(8,128)} fusion(bf16[2,1024,512]{2,1,0:T(8,128)(2,1)S(1)} %bitcast.40, bf16[1,256,1,512]{3,0,1,2:T(2,128)(2,1)S(1)} %constant_dynamic-slice_fusion), kind=kOutput, calls=%fused_computation.1 | convolution fusion | flops 537395200 | bytes 4456448 | tf_op jit(solution)/shard_map/cik,cjk->cij/dot_general | solution.py:42
  (5 shorter events, 0.1 us)
Async XLA Ops:
  6.5 43.2 %all-gather.3.cloned.1.call-start = ((), (), s32[]{:S(2)}) async-start(), calls=%async_computation.1 | async-start | bytes 1310720 | tf_op jit(solution)/shard_map/all_gather | solution.py:59
  53.0 72.0 %all-to-all-start = ((bf16[4,2,128,512]{3,1,0,2:T(2,128)(2,1)}), bf16[4,2,128,512]{3,1,0,2:T(2,128)(2,1)S(1)}, u32[]{:S(2)}, u32[]{:S(2)}) async-start(bf16[4,2,128,512]{3,1,0,2:T(2,128)(2,1)} %copy.17), calls=%async_computation | async-start | bytes 2097152 | tf_op jit(solution)/shard_map/all_to_all | solution.py:60
Sparse Core Ops, SparseCore 0:
  15.6 34.0 all-gather.2
where the time goes:
time: 146 us; the launch traced here: 144 us
  waiting for transfers between devices  87.3 us (60%)
  starting transfers between devices  18.9 us (13%)
  between operations  13.5 us (9%)
  local copies, waits for them, and re-layouts  10.5 us (7%)
  other arithmetic  8.5 us (6%)
  matrix products  5.56 us (4%)
    all_to_all x1, waiting for transfers between devices, shards(): lax.all_to_all(gathered, 'chan', split_axis=2, concat_axis=1, tiled=True)  53.1 us
    all_gather x1, waiting for transfers between devices, shards(): gathered = lax.all_gather(spectra, 'pair', axis=0, tiled=True)  34.2 us
    all_to_all x1, starting transfers between devices, shards(): lax.all_to_all(gathered, 'chan', split_axis=2, concat_axis=1, tiled=True)  18.9 us
    dot_general x2, matrix products, channelize(): jnp.einsum('wn,asn->aws', transform, filtered, precision=lax.Precision.HI...  3.49 us
    all_gather x1, local copies, waits for them, and re-layouts, shards(): gathered = lax.all_gather(spectra, 'pair', axis=0, tiled=True)  3.27 us
  transfers between devices with their start and end apart: 2, of which 2 were waited for; matrix products, arithmetic and copies ran while one was open for 0% of the time, Pallas kernels for 0%

commit v1 on v0

v1 whole, which is shorter than its diff:
```python
import functools
import math

import jax
import jax.numpy as jnp
import ml_dtypes
import numpy as np
from jax import lax
from jax.experimental import pallas as pl
from jax.experimental.pallas import tpu as pltpu
from jax.sharding import PartitionSpec as P

MESH = pl.DeviceIdType.MESH
NY, NZ, NX = 4, 16, 2
FAR_FIRST = True


def dft_matrix(channels):
    frame = 2 * channels
    part, y, x, z = np.meshgrid(np.arange(2), np.arange(NY), np.arange(NX), np.arange(NZ), indexing="ij")
    freq = ((y * NZ + z) * NX + x).reshape(-1)
    part = part.reshape(-1)
    phases = freq[:, None] * np.arange(frame)[None, :] % frame
    angles = phases * (2.0 * math.pi / frame)
    full = np.where((part == 0)[:, None], np.cos(angles), -np.sin(angles)) / math.sqrt(frame)
    full = full.astype(np.float32)
    high = full.astype(ml_dtypes.bfloat16)
    low = (full - high.astype(np.float32)).astype(ml_dtypes.bfloat16)
    return high, low


def split(value):
    high = value.astype(jnp.bfloat16)
    return high, (value - high.astype(jnp.float32)).astype(jnp.bfloat16)


def nt_dot(a, b):
    return lax.dot_general(a, b, (((1,), (1,)), ((), ())), preferred_element_type=jnp.float32)


def channelize_kernel(volt_ref, taps_ref, high_ref, low_ref, out_ref, wide, filt, inter):
    taps, frame = taps_ref.shape
    half = frame // 2
    frames = volt_ref.shape[0] // 8
    spectra = frames - taps + 1
    wide[...] = volt_ref[...].astype(jnp.float32)
    row = lax.broadcasted_iota(jnp.int32, (8, half), 0)
    second = (row // 2) % 2 == 1
    pattern = []
    for p in range(taps):
        first_half = jnp.broadcast_to(taps_ref[p : p + 1, :half], (8, half))
        other_half = jnp.broadcast_to(taps_ref[p : p + 1, half:], (8, half))
        pattern.append(jnp.where(second, other_half, first_half)[None])
    block = 128
    for j in range(2):
        for part in range(4 * spectra // block):
            base = j * 4 * frames + part * block
            total = None
            for p in range(taps):
                rows = wide[base + 4 * p : base + 4 * p + block, :].reshape(block // 8, 8, half)
                term = rows * pattern[p]
                total = term if total is None else total + term
            at = (j * 4 * spectra) + part * block
            filt[at : at + block, :] = total.reshape(block, half)
    columns = []
    for b in range(2):
        for j in range(2):
            start = j * 4 * spectra + b
            columns.append(
                jnp.concatenate(
                    [
                        filt[pl.ds(start, spectra, stride=4), :],
                        filt[pl.ds(start + 2, spectra, stride=4), :],
                    ],
                    axis=1,
                )
            )
    frames_high, frames_low = split(jnp.concatenate(columns, axis=0))
    high, low = high_ref[...], low_ref[...]
    result = nt_dot(high, frames_high) + (nt_dot(high, frames_low) + nt_dot(low, frames_high))
    channels = high.shape[0] // 2
    for b in range(2):
        for part in range(2):
            for j in range(2):
                at = (b * 2 + part) * 2 * channels + j
                column = (b * 2 + j) * spectra
                inter[pl.ds(at, channels, stride=2), :] = result[
                    part * channels : (part + 1) * channels, column : column + spectra
                ]
    out_ref[...] = inter[...].astype(jnp.bfloat16)


def exchange_kernel(
    src, out, near, local_sem, b_send, b_recv, a_send, a_recv, core_send, core_recv, x_send, x_recv, on_send, on_recv
):
    chan, pair = lax.axis_index("chan"), lax.axis_index("pair")
    y, z, x = chan // (NZ * NX), (chan // NX) % NZ, chan % NX
    core_mate = pair + 1 - 2 * (pair % 2)
    x_mate = (pair + 2) % 4

    def chan_of(y, z, x):
        return (y * NZ + z) * NX + x

    groups = NY * NX
    barrier = pltpu.get_barrier_semaphore()

    def greet(c, p):
        pl.semaphore_signal(barrier, inc=1, device_id={"chan": c, "pair": p}, device_id_type=MESH)

    def other(t):
        d = (y * NX + x + t) % groups
        return d // NX, d % NX

    def step_offset(t):
        t = NZ - 2 - t if FAR_FIRST else t
        m = t // 2 + 1
        return jnp.where(t % 2 == 0, m, NZ - m)

    for t in range(1, groups):
        oy, ox = other(t)
        greet(chan_of(oy, z, ox), pair)
    for t in range(1, NZ):
        greet(chan_of(y, (z + t) % NZ, x), pair)
    greet(chan, core_mate)
    greet(chan, x_mate)
    pl.semaphore_wait(barrier, groups - 1 + NZ - 1 + 2)

    def b_copy(t):
        oy, ox = other(t)
        return pltpu.make_async_remote_copy(
            src_ref=src.at[:, oy, ox],
            dst_ref=near.at[:, y, :, x],
            send_sem=b_send.at[t],
            recv_sem=b_recv.at[t],
            device_id={"chan": chan_of(oy, z, ox), "pair": pair},
            device_id_type=MESH,
        )

    def b_arrival(t):
        d = (y * NX + x - t + groups) % groups
        oy, ox = d // NX, d % NX
        return pltpu.make_async_remote_copy(
            src_ref=src.at[:, oy, ox],
            dst_ref=near.at[:, oy, :, ox],
            send_sem=b_send.at[t],
            recv_sem=b_recv.at[t],
            device_id={"chan": chan_of(oy, z, ox), "pair": pair},
            device_id_type=MESH,
        )

    own = pltpu.make_async_copy(src.at[:, y, x], near.at[:, y, :, x], local_sem.at[0])
    for t in range(1, groups):
        b_copy(t).start()
    own.start()
    own.wait()
    for t in range(1, groups):
        b_arrival(t).wait_recv()

    def a_copy(t):
        oz = (z + step_offset(t)) % NZ
        return pltpu.make_async_remote_copy(
            src_ref=near.at[:, :, oz],
            dst_ref=out.at[:, pair, :, z],
            send_sem=a_send.at[t],
            recv_sem=a_recv.at[t],
            device_id={"chan": chan_of(y, oz, x), "pair": pair},
            device_id_type=MESH,
        )

    def source(t):
        return (z - step_offset(t) + NZ) % NZ

    def a_arrival(t):
        oz = source(t)
        return pltpu.make_async_remote_copy(
            src_ref=near.at[:, :, oz],
            dst_ref=out.at[:, pair, :, oz],
            send_sem=a_send.at[t],
            recv_sem=a_recv.at[t],
            device_id={"chan": chan_of(y, oz, x), "pair": pair},
            device_id_type=MESH,
        )

    def pass_on(block, at, target, send, recv, t):
        return pltpu.make_async_remote_copy(
            src_ref=out.at[:, block, :, at],
            dst_ref=out.at[:, block, :, at],
            send_sem=send.at[t],
            recv_sem=recv.at[t],
            device_id={"chan": chan, "pair": target},
            device_id_type=MESH,
        )

    own_z = pltpu.make_async_copy(near.at[:, :, z], out.at[:, pair, :, z], local_sem.at[1])
    own_z.start()

    @pl.loop(0, NZ - 1)
    def _(t):
        a_copy(t).start()

    own_z.wait()
    pass_on(pair, z, x_mate, x_send, x_recv, NZ - 1).start()
    pass_on(pair, z, core_mate, core_send, core_recv, NZ - 1).start()

    @pl.loop(0, NZ - 1)
    def _(t):
        a_arrival(t).wait_recv()
        pass_on(pair, source(t), x_mate, x_send, x_recv, t).start()
        pass_on(pair, source(t), core_mate, core_send, core_recv, t).start()
        previous = (t + NZ - 1) % NZ
        at = jnp.where(t == 0, z, source(previous))
        pass_on(x_mate, at, x_mate, x_send, x_recv, previous).wait_recv()
        pass_on(x_mate, at, core_mate, on_send, on_recv, previous).start()

    last = NZ - 2
    pass_on(x_mate, source(last), x_mate, x_send, x_recv, last).wait_recv()
    pass_on(x_mate, source(last), core_mate, on_send, on_recv, last).start()

    diagonal = (core_mate + 2) % 4

    @pl.loop(0, NZ)
    def _(t):
        at = jnp.where(t == NZ - 1, z, source(t))
        pass_on(core_mate, at, core_mate, core_send, core_recv, t).wait_recv()
        pass_on(diagonal, at, core_mate, on_send, on_recv, t).wait_recv()
        pass_on(pair, at, core_mate, core_send, core_recv, t).wait_send()
        pass_on(pair, at, x_mate, x_send, x_recv, t).wait_send()
        pass_on(x_mate, at, core_mate, on_send, on_recv, t).wait_send()

    @pl.loop(0, NZ - 1)
    def _(t):
        a_copy(t).wait_send()

    for t in range(1, groups):
        b_copy(t).wait_send()


def correlate_kernel(scale, rows_ref, own_ref, out_ref):
    wide = [rows_ref[q] for q in range(4)]
    own = [own_ref[q] for q in range(4)]
    columns = jnp.concatenate(wide, axis=1)
    straight = jnp.concatenate(own, axis=1)
    turned = jnp.concatenate([own[1], -own[0], own[3], -own[2]], axis=1)
    out_ref[0] = nt_dot(straight, columns) * scale
    out_ref[1] = nt_dot(turned, columns) * scale


def shards(voltages, fir_taps):
    _, antennas, batches, samples = voltages.shape
    taps, frame = fir_taps.shape
    frames = samples // frame
    spectra_len = frames - taps + 1
    half = frame // 2
    volt = voltages.reshape(antennas, batches, samples // half, half)
    volt = jnp.transpose(volt, (0, 2, 1, 3)).reshape(antennas * batches * samples // half, half)
    high, low = dft_matrix(half)
    vmem = pl.BlockSpec(memory_space=pltpu.VMEM)
    spectra = pl.pallas_call(
        channelize_kernel,
        out_shape=jax.ShapeDtypeStruct((8 * half, spectra_len), jnp.bfloat16),
        in_specs=[vmem] * 4,
        out_specs=vmem,
        scratch_shapes=[
            pltpu.VMEM(volt.shape, jnp.float32),
            pltpu.VMEM((8 * spectra_len, half), jnp.float32),
            pltpu.VMEM((8 * half, spectra_len), jnp.float32),
        ],
        compiler_params=pltpu.CompilerParams(vmem_limit_bytes=16 * 1024 * 1024),
    )(volt, fir_taps, jnp.asarray(high), jnp.asarray(low))
    spectra = spectra.reshape(4, NY, NX, NZ, 2, spectra_len)
    dma = pltpu.SemaphoreType.DMA
    everyone = pl.pallas_call(
        exchange_kernel,
        out_shape=jax.ShapeDtypeStruct((4, 4, NY, NZ, NX, 2, spectra_len), jnp.bfloat16),
        in_specs=[pl.BlockSpec(memory_space=pl.ANY)],
        out_specs=pl.BlockSpec(memory_space=pl.ANY),
        scratch_shapes=[
            pltpu.VMEM((4, NY, NZ, NX, 2, spectra_len), jnp.bfloat16),
            dma((2,)),
            dma((NY * NX,)),
            dma((NY * NX,)),
        ]
        + [dma((NZ,))] * 8,
        compiler_params=pltpu.CompilerParams(
            collective_id=0, has_side_effects=True, vmem_limit_bytes=16 * 1024 * 1024
        ),
    )(spectra)
    everyone = everyone.reshape(4, 4 * NY * NZ * NX * 2, spectra_len)
    total = everyone.shape[1]
    block = total // 4
    tile = 256
    index = lax.axis_index("pair")
    scale = 1.0 / math.sqrt(batches * spectra_len)
    own_rows = lax.dynamic_slice_in_dim(everyone, index * block, block, axis=1)
    return pl.pallas_call(
        functools.partial(correlate_kernel, scale),
        grid=(total // tile,),
        out_shape=jax.ShapeDtypeStruct((1, 2, block, total), jnp.float32),
        in_specs=[
            pl.BlockSpec((4, tile, spectra_len), lambda g: (0, g, 0)),
            pl.BlockSpec((4, block, spectra_len), lambda g: (0, 0, 0)),
        ],
        out_specs=pl.BlockSpec((None, 2, block, tile), lambda g: (0, 0, 0, g)),
        compiler_params=pltpu.CompilerParams(vmem_limit_bytes=16 * 1024 * 1024),
    )(everyone, own_rows)


def solution(mesh):
    in_specs = (P("pair", "chan", None, None), P())
    out_specs = P("chan", None, "pair", None)
    return jax.shard_map(shards, mesh=mesh, in_specs=in_specs, out_specs=out_specs, check_vma=False)
```

time: 146 us -> 63.6 us (0.44); the launches traced: 144 us -> 63.3 us
  waiting for transfers between devices: 87.3 us -> 0 us
  Pallas kernels: 0 us -> 59.4 us
  starting transfers between devices: 18.9 us -> 0 us
  between operations: 13.5 us -> 0.05 us
  other arithmetic: 8.5 us -> 0 us
  local copies, waits for them, and re-layouts: 10.5 us -> 3.87 us
  matrix products: 5.56 us -> 0 us
    pallas_call x0 -> x3, Pallas kernels: none -> 59.4 us  [the longest x1 56 us: shards(): pl.pallas_call(exchange_kernel, out_shape=jax.ShapeDtypeStruct((4, 4, NY,...]
    all_to_all x1 -> x0, waiting for transfers between devices: 53.1 us -> none  [shards(): lax.all_to_all(gathered, 'chan', split_axis=2, concat_axis=1, tiled=True)]
    all_gather x1 -> x0, waiting for transfers between devices: 34.2 us -> none  [shards(): gathered = lax.all_gather(spectra, 'pair', axis=0, tiled=True)]
    all_to_all x1 -> x0, starting transfers between devices: 18.9 us -> none  [shards(): lax.all_to_all(gathered, 'chan', split_axis=2, concat_axis=1, tiled=True)]
    dot_general x3 -> x0, matrix products: 5.56 us -> none  [the longest x2 3.49 us: channelize(): jnp.einsum('wn,asn->aws', transform, filtered, precision=lax.Precision.HI...]
    all_gather x1 -> x0, local copies, waits for them, and re-layouts: 3.27 us -> none  [shards(): gathered = lax.all_gather(spectra, 'pair', axis=0, tiled=True)]
    convert_element_type x1 -> x0, other arithmetic: 2.85 us -> none  [channelize(): sample_rows.astype(jnp.float32)]
    unnamed x0 -> x6, local copies, waits for them, and re-layouts: none -> 2.5 us
  transfers between devices with their start and end apart: 2 -> 0, of which waited for: 2 -> 0; matrix products, arithmetic and copies ran while one was open for 0% -> 0% of each run, Pallas kernels for 0% -> 0%
where the time goes in v1:
time: 63.6 us; the launch traced here: 63.3 us
  Pallas kernels  59.4 us (93%)
  local copies, waits for them, and re-layouts  3.87 us (6%)
    pallas_call x1, Pallas kernels, shards(): pl.pallas_call(exchange_kernel, out_shape=jax.ShapeDtypeStruct((4, 4, NY,...  56 us
    pallas_call x1, Pallas kernels, shards(): pl.pallas_call(functools.partial(correlate_kernel, scale), grid=(total //...  2.68 us
    unnamed x6, local copies, waits for them, and re-layouts  2.5 us

profile of v1, /device:TPU:1, one launch (start us, length us, event | category | flops | bytes accessed | tf_op | source)
XLA Modules:
  0.0 63.3 jit_solution(9761834455858595907)
XLA Ops:
  0.0 1.1 %reshape.12 = bf16[2,2,270,128]{3,2,1,0:T(8,128)(2,1)S(1)} reshape(bf16[1,2,2,34560]{3,2,1,0:T(2,128)(2,1)} %param.4) | data formatting | bytes 552960 | tf_op jit(solution)/shard_map/reshape | solution.py:254
  1.1 0.2 copy.6
  1.4 0.0 copy-start
  1.4 0.9 %copy-done = bf16[256,256]{1,0:T(8,128)(2,1)S(1)} copy-done((bf16[256,256]{1,0:T(8,128)(2,1)S(1)}, bf16[256,256]{1,0:T(8,128)(2,1)}, u32[]{:S(2)}) %copy-start) | copy-done | bytes 131096
  2.3 0.0 copy-start.1
  2.3 0.9 %copy-done.1 = bf16[256,256]{1,0:T(8,128)(2,1)S(1)} copy-done((bf16[256,256]{1,0:T(8,128)(2,1)S(1)}, bf16[256,256]{1,0:T(8,128)(2,1)}, u32[]{:S(2)}) %copy-start.1) | copy-done | bytes 131096
  3.2 0.0 copy-start.2
  3.2 0.7 %copy-done.2 = f32[8,256]{1,0:T(8,128)S(1)} copy-done((f32[8,256]{1,0:T(8,128)S(1)}, f32[8,256]{1,0:T(8,128)}, u32[]{:S(2)}) %copy-start.2) | copy-done | bytes 8216
  3.9 0.7 %shard_map.46 = bf16[1024,128]{1,0:T(8,128)(2,1)S(1)} custom-call(bf16[1080,128]{1,0:T(8,128)(2,1)S(1)} %bitcast.6, f32[8,256]{1,0:T(8,128)S(1)} %copy-done.2, bf16[256,256]{1,0:T(8,128)(2,1)S(1)} %copy-done.1, bf16[256,256]{1,0:T(8,128)(2,1)S(1)} %copy-done), custom_call_target="tpu_custom_call" | custom-call | tf_op jit(solution)/shard_map/pallas_call | solution.py:258
  4.6 56.0 %shard_map.47 = bf16[4,4,4,16,2,2,128]{6,5,4,3,2,1,0:T(2,128)(2,1)S(1)} custom-call(bf16[4,4,2,16,2,128]{5,4,3,2,1,0:T(2,128)(2,1)S(1)} %bitcast.7), custom_call_target="tpu_custom_call" | custom-call | tf_op jit(solution)/shard_map/pallas_call | solution.py:272
  60.7 2.7 %shard_map.48 = f32[1,2,256,1024]{3,2,1,0:T(8,128)} custom-call(bf16[4,1024,128]{2,1,0:T(8,128)(2,1)S(1)} %bitcast.5, bf16[4,256,128]{2,1,0:T(8,128)(2,1)S(1)} %constant_dynamic-slice_fusion.own_ref), custom_call_target="tpu_custom_call" | custom-call | tf_op jit(solution)/shard_map/pallas_call | solution.py:295
  (1 shorter events, 0.0 us)
Async XLA Ops:
  1.4 0.9 %copy-start = (bf16[256,256]{1,0:T(8,128)(2,1)S(1)}, bf16[256,256]{1,0:T(8,128)(2,1)}, u32[]{:S(2)}) copy-start(bf16[256,256]{1,0:T(8,128)(2,1)} %constant.15.clone.low_ref) | copy-start | bytes 393220
  2.3 0.9 %copy-start.1 = (bf16[256,256]{1,0:T(8,128)(2,1)S(1)}, bf16[256,256]{1,0:T(8,128)(2,1)}, u32[]{:S(2)}) copy-start(bf16[256,256]{1,0:T(8,128)(2,1)} %constant.14.clone.high_ref) | copy-start | bytes 393220
  3.2 0.7 %copy-start.2 = (f32[8,256]{1,0:T(8,128)S(1)}, f32[8,256]{1,0:T(8,128)}, u32[]{:S(2)}) copy-start(f32[8,256]{1,0:T(8,128)} %taps_ref.1) | copy-start | bytes 24580

commit v2 on v0

v2 whole, which is shorter than its diff:
```python
import functools
import math

import jax
import jax.numpy as jnp
import ml_dtypes
import numpy as np
from jax import lax
from jax.experimental import pallas as pl
from jax.experimental.layout import Layout, with_layout_constraint
from jax.experimental.pallas import tpu as pltpu
from jax.sharding import PartitionSpec as P

MESH = pl.DeviceIdType.MESH
NY, NZ, NX = 4, 16, 2
QUADS = NZ // 4
GROUPS = NY * NX
VMEM_LIMIT = 56 * 1024 * 1024
Z_STEPS = (
    [(2, k) for k in range(4)]
    + [(r, k) for k in range(4) for r in (1, 3)]
    + [(0, k) for k in range(1, 4)]
)
QUAD_ORDER = (2, 1, 3, 0)


def dft_matrix(channels):
    frame = 2 * channels
    part, y, x, z = np.meshgrid(np.arange(2), np.arange(NY), np.arange(NX), np.arange(NZ), indexing="ij")
    freq = ((y * NZ + z) * NX + x).reshape(-1)
    part = part.reshape(-1)
    phases = freq[:, None] * np.arange(frame)[None, :] % frame
    angles = phases * (2.0 * math.pi / frame)
    full = np.where((part == 0)[:, None], np.cos(angles), -np.sin(angles)) / math.sqrt(frame)
    full = full.astype(np.float32)
    high = full.astype(ml_dtypes.bfloat16)
    low = (full - high.astype(np.float32)).astype(ml_dtypes.bfloat16)
    return high, low


def split(value):
    high = value.astype(jnp.bfloat16)
    return high, (value - high.astype(jnp.float32)).astype(jnp.bfloat16)


def nt_dot(a, b):
    return lax.dot_general(a, b, (((1,), (1,)), ((), ())), preferred_element_type=jnp.float32)


def channelize(volt, taps_ref, high_ref, low_ref, spec, wide, filt, inter):
    taps, frame = taps_ref.shape
    half = frame // 2
    frames = volt.shape[0] // 8
    spectra = frames - taps + 1
    wide[...] = volt[...].astype(jnp.float32)
    row = lax.broadcasted_iota(jnp.int32, (8, half), 0)
    second = (row // 2) % 2 == 1
    pattern = []
    for p in range(taps):
        first_half = jnp.broadcast_to(taps_ref[p : p + 1, :half], (8, half))
        other_half = jnp.broadcast_to(taps_ref[p : p + 1, half:], (8, half))
        pattern.append(jnp.where(second, other_half, first_half)[None])
    block = 128
    for j in range(2):
        for part in range(4 * spectra // block):
            base = j * 4 * frames + part * block
            total = None
            for p in range(taps):
                rows = wide[base + 4 * p : base + 4 * p + block, :].reshape(block // 8, 8, half)
                term = rows * pattern[p]
                total = term if total is None else total + term
            at = (j * 4 * spectra) + part * block
            filt[at : at + block, :] = total.reshape(block, half)
    columns = []
    for b in range(2):
        for j in range(2):
            start = j * 4 * spectra + b
            columns.append(
                jnp.concatenate(
                    [
                        filt[pl.ds(start, spectra, stride=4), :],
                        filt[pl.ds(start + 2, spectra, stride=4), :],
                    ],
                    axis=1,
                )
            )
    frames_high, frames_low = split(jnp.concatenate(columns, axis=0))
    high, low = high_ref[...], low_ref[...]
    result = nt_dot(high, frames_high) + (nt_dot(high, frames_low) + nt_dot(low, frames_high))
    channels = high.shape[0] // 2
    for b in range(2):
        for part in range(2):
            for j in range(2):
                column = (b * 2 + j) * spectra
                inter[b, part, :, j, :] = result[
                    part * channels : (part + 1) * channels, column : column + spectra
                ]
    for b in range(2):
        for part in range(2):
            spec[b, part] = (
                inter[b, part].astype(jnp.bfloat16).reshape(NY, NX, NZ, 2, spectra)
            )


def spread_kernel(
    volt_hbm, taps_hbm, high_hbm, low_hbm, out,
    volt, taps, high, low, wide, filt, inter, spec, near,
    load_sem, own_sem, b_send, b_recv, a_send, a_recv, core_send, core_recv, x_send, x_recv, on_send, on_recv,
):
    loads = [
        pltpu.make_async_copy(source, target, load_sem.at[i])
        for i, (source, target) in enumerate(((volt_hbm, volt), (taps_hbm, taps), (high_hbm, high), (low_hbm, low)))
    ]
    for load in loads:
        load.start()

    chan, pair = lax.axis_index("chan"), lax.axis_index("pair")
    y, z, x = chan // (NZ * NX), (chan // NX) % NZ, chan % NX
    quad, place = z // 4, z % 4
    core_mate = pair + 1 - 2 * (pair % 2)
    x_mate = (pair + 2) % 4

    def chan_of(y, z, x):
        return (y * NZ + z) * NX + x

    def group_ahead(t):
        d = (y * NX + x + t) % GROUPS
        return d // NX, d % NX

    def z_ahead(r, k):
        return (quad + r) % QUADS * 4 + (place + k) % 4

    def z_behind(r, k):
        return (quad - r + QUADS) % QUADS * 4 + (place - k + 4) % 4

    barrier = pltpu.get_barrier_semaphore()

    def greet(c, p):
        pl.semaphore_signal(barrier, inc=1, device_id={"chan": c, "pair": p}, device_id_type=MESH)

    for r, k in Z_STEPS:
        greet(chan_of(y, z_ahead(r, k), x), pair)
    for t in range(1, GROUPS):
        oy, ox = group_ahead(t)
        greet(chan_of(oy, z, ox), pair)
    greet(chan, x_mate)
    greet(chan, core_mate)

    for load in loads:
        load.wait()
    channelize(volt, taps, high, low, spec, wide, filt, inter)
    pl.semaphore_wait(barrier, len(Z_STEPS) + GROUPS - 1 + 2)

    def remote(source, target, send, recv, c, p):
        return pltpu.make_async_remote_copy(
            src_ref=source, dst_ref=target, send_sem=send, recv_sem=recv,
            device_id={"chan": c, "pair": p}, device_id_type=MESH,
        )

    def b_copy(b, t):
        oy, ox = group_ahead(t)
        return remote(
            spec.at[b, :, oy, ox], near.at[b, :, y, :, x],
            b_send.at[b, t], b_recv.at[b, t], chan_of(oy, z, ox), pair,
        )

    def b_arrival(b, t):
        oy, ox = group_ahead(GROUPS - t)
        return remote(
            spec.at[b, :, oy, ox], near.at[b, :, oy, :, ox],
            b_send.at[b, t], b_recv.at[b, t], chan_of(oy, z, ox), pair,
        )

    def a_copy(b, r, k):
        oz = z_ahead(r, k)
        return remote(
            near.at[b, :, :, oz], out.at[b, :, pair, :, z],
            a_send.at[b, r * 4 + k], a_recv.at[b, r * 4 + k], chan_of(y, oz, x), pair,
        )

    def a_arrival(b, r, k):
        oz = z_behind(r, k)
        return remote(
            near.at[b, :, :, oz], out.at[b, :, pair, :, oz],
            a_send.at[b, r * 4 + k], a_recv.at[b, r * 4 + k], chan_of(y, oz, x), pair,
        )

    def pass_on(b, block, r, target, send, recv):
        at = pl.ds((quad - r + QUADS) % QUADS * 4, 4)
        ref = out.at[b, :, block, :, at]
        return remote(ref, ref, send.at[b, r], recv.at[b, r], chan, target)

    own = [pltpu.make_async_copy(spec.at[b, :, y, x], near.at[b, :, y, :, x], own_sem.at[b]) for b in range(2)]
    own_z = [pltpu.make_async_copy(near.at[b, :, :, z], out.at[b, :, pair, :, z], own_sem.at[2 + b]) for b in range(2)]

    for b in range(2):
        for t in range(1, GROUPS):
            b_copy(b, t).start()
        own[b].start()
    for b in range(2):
        own[b].wait()
        for t in range(1, GROUPS):
            b_arrival(b, t).wait_recv()
        for r, k in Z_STEPS:
            a_copy(b, r, k).start()
        own_z[b].start()

    def gather(b, r):
        for k in range(4):
            if r or k:
                a_arrival(b, r, k).wait_recv()
        if r == 0:
            own_z[b].wait()
        pass_on(b, pair, r, x_mate, x_send, x_recv).start()
        pass_on(b, pair, r, core_mate, core_send, core_recv).start()

    def forward(b, r):
        pass_on(b, x_mate, r, x_mate, x_send, x_recv).wait_recv()
        pass_on(b, x_mate, r, core_mate, on_send, on_recv).start()

    for r in QUAD_ORDER:
        gather(0, r)
    for r in QUAD_ORDER:
        forward(0, r)
        gather(1, r)
    for r in QUAD_ORDER:
        forward(1, r)

    diagonal = (core_mate + 2) % 4
    for b in range(2):
        for r in range(QUADS):
            pass_on(b, core_mate, r, core_mate, core_send, core_recv).wait_recv()
            pass_on(b, diagonal, r, core_mate, on_send, on_recv).wait_recv()
            pass_on(b, pair, r, core_mate, core_send, core_recv).wait_send()
            pass_on(b, pair, r, x_mate, x_send, x_recv).wait_send()
            pass_on(b, x_mate, r, core_mate, on_send, on_recv).wait_send()
        for r, k in Z_STEPS:
            a_copy(b, r, k).wait_send()
        for t in range(1, GROUPS):
            b_copy(b, t).wait_send()


def correlate_kernel(scale, everyone, out, held, own, result, in_sem, out_sem):
    tiles, _, block, tile = result.shape
    mine = pl.ds(pl.multiple_of(lax.axis_index("pair") * block, block), block)
    own_load = pltpu.make_async_copy(everyone.at[:, mine], own, in_sem.at[tiles])
    own_load.start()
    loads, stores = [], []
    for g in range(tiles):
        there = pl.ds(g * tile, tile)
        loads.append(pltpu.make_async_copy(everyone.at[:, there], held.at[g], in_sem.at[g]))
        stores.append(pltpu.make_async_copy(result.at[g], out.at[0, :, :, there], out_sem.at[g]))
        loads[g].start()
    own_load.wait()
    rows = [own[q] for q in range(4)]
    straight = jnp.concatenate(rows, axis=1)
    turned = jnp.concatenate([rows[1], -rows[0], rows[3], -rows[2]], axis=1)
    for g in range(tiles):
        loads[g].wait()
        columns = jnp.concatenate([held[g, q] for q in range(4)], axis=1)
        result[g, 0] = nt_dot(straight, columns) * scale
        result[g, 1] = nt_dot(turned, columns) * scale
        stores[g].start()
    for store in stores:
        store.wait()


def shards(voltages, fir_taps):
    _, antennas, batches, samples = voltages.shape
    taps, frame = fir_taps.shape
    frames = samples // frame
    spectra_len = frames - taps + 1
    half = frame // 2
    volt = voltages.reshape(antennas, batches, samples // half, half)
    volt = with_layout_constraint(volt, Layout(major_to_minor=(0, 2, 1, 3)))
    volt = jnp.transpose(volt, (0, 2, 1, 3)).reshape(antennas * batches * samples // half, half)
    high, low = dft_matrix(half)
    hbm = pl.BlockSpec(memory_space=pltpu.HBM)
    dma = pltpu.SemaphoreType.DMA
    everyone = pl.pallas_call(
        spread_kernel,
        out_shape=jax.ShapeDtypeStruct((2, 2, 4, NY, NZ, NX, 2, spectra_len), jnp.bfloat16),
        in_specs=[hbm] * 4,
        out_specs=hbm,
        scratch_shapes=[
            pltpu.VMEM(volt.shape, jnp.bfloat16),
            pltpu.VMEM(fir_taps.shape, jnp.float32),
            pltpu.VMEM(high.shape, jnp.bfloat16),
            pltpu.VMEM(low.shape, jnp.bfloat16),
            pltpu.VMEM(volt.shape, jnp.float32),
            pltpu.VMEM((8 * spectra_len, half), jnp.float32),
            pltpu.VMEM((2, 2, half, 2, spectra_len), jnp.float32),
            pltpu.VMEM((2, 2, NY, NX, NZ, 2, spectra_len), jnp.bfloat16),
            pltpu.VMEM((2, 2, NY, NZ, NX, 2, spectra_len), jnp.bfloat16),
            dma((4,)),
            dma((4,)),
            dma((2, GROUPS)),
            dma((2, GROUPS)),
            dma((2, NZ)),
            dma((2, NZ)),
        ]
        + [dma((2, QUADS))] * 6,
        compiler_params=pltpu.CompilerParams(
            collective_id=0, has_side_effects=True, vmem_limit_bytes=VMEM_LIMIT
        ),
    )(volt, fir_taps, jnp.asarray(high), jnp.asarray(low))
    everyone = everyone.reshape(4, 4 * NY * NZ * NX * 2, spectra_len)
    total = everyone.shape[1]
    block = total // 4
    tiles = 4
    tile = total // tiles
    scale = 1.0 / math.sqrt(batches * spectra_len)
    return pl.pallas_call(
        functools.partial(correlate_kernel, scale),
        out_shape=jax.ShapeDtypeStruct((1, 2, block, total), jnp.float32),
        in_specs=[hbm],
        out_specs=hbm,
        scratch_shapes=[
            pltpu.VMEM((tiles, 4, tile, spectra_len), jnp.bfloat16),
            pltpu.VMEM((4, block, spectra_len), jnp.bfloat16),
            pltpu.VMEM((tiles, 2, block, tile), jnp.float32),
            dma((tiles + 1,)),
            dma((tiles,)),
        ],
        compiler_params=pltpu.CompilerParams(vmem_limit_bytes=VMEM_LIMIT),
    )(everyone)


def solution(mesh):
    in_specs = (P("pair", "chan", None, None), P())
    out_specs = P("chan", None, "pair", None)
    return jax.shard_map(shards, mesh=mesh, in_specs=in_specs, out_specs=out_specs, check_vma=False)
```

time: 146 us -> 46.9 us (0.32); the launches traced: 144 us -> 46.8 us
  waiting for transfers between devices: 87.3 us -> 0 us
  Pallas kernels: 0 us -> 46.8 us
  starting transfers between devices: 18.9 us -> 0 us
  between operations: 13.5 us -> 0.01 us
  local copies, waits for them, and re-layouts: 10.5 us -> 0 us
  other arithmetic: 8.5 us -> 0 us
  matrix products: 5.56 us -> 0 us
    all_to_all x1 -> x0, waiting for transfers between devices: 53.1 us -> none  [shards(): lax.all_to_all(gathered, 'chan', split_axis=2, concat_axis=1, tiled=True)]
    pallas_call x0 -> x2, Pallas kernels: none -> 46.8 us  [the longest x1 43.5 us: shards(): pl.pallas_call(spread_kernel, out_shape=jax.ShapeDtypeStruct((2, 2, 4, NY...]
    all_gather x1 -> x0, waiting for transfers between devices: 34.2 us -> none  [shards(): gathered = lax.all_gather(spectra, 'pair', axis=0, tiled=True)]
    all_to_all x1 -> x0, starting transfers between devices: 18.9 us -> none  [shards(): lax.all_to_all(gathered, 'chan', split_axis=2, concat_axis=1, tiled=True)]
    dot_general x3 -> x0, matrix products: 5.56 us -> none  [the longest x2 3.49 us: channelize(): jnp.einsum('wn,asn->aws', transform, filtered, precision=lax.Precision.HI...]
    all_gather x1 -> x0, local copies, waits for them, and re-layouts: 3.27 us -> none  [shards(): gathered = lax.all_gather(spectra, 'pair', axis=0, tiled=True)]
    convert_element_type x1 -> x0, other arithmetic: 2.85 us -> none  [channelize(): sample_rows.astype(jnp.float32)]
    another operation x1 -> x0, other arithmetic: 2.43 us -> none  [correlate(): jnp.stack([-shaped[:, :, :, 1, :], shaped[:, :, :, 0, :]], axis=3)]
  transfers between devices with their start and end apart: 2 -> 0, of which waited for: 2 -> 0; matrix products, arithmetic and copies ran while one was open for 0% -> 0% of each run, Pallas kernels for 0% -> 0%
where the time goes in v2:
time: 46.9 us; the launch traced here: 46.8 us
  Pallas kernels  46.8 us (100%)
    pallas_call x1, Pallas kernels, shards(): pl.pallas_call(spread_kernel, out_shape=jax.ShapeDtypeStruct((2, 2, 4, NY...  43.5 us
    pallas_call x1, Pallas kernels, shards(): pl.pallas_call(functools.partial(correlate_kernel, scale), out_shape=jax....  3.25 us

profile of v2, /device:TPU:1, one launch (start us, length us, event | category | flops | bytes accessed | tf_op | source)
XLA Modules:
  0.0 46.8 jit_solution(10819561139777826490)
XLA Ops:
  0.0 43.5 %shard_map.46 = bf16[2,2,4,4,16,2,2,128]{7,6,5,4,3,2,1,0:T(2,128)(2,1)} custom-call(bf16[1080,128]{1,0:T(8,128)(2,1)} %bitcast.7, f32[8,256]{1,0:T(8,128)} %taps_hbm.1, bf16[256,256]{1,0:T(8,128)(2,1)} %constant.4.clone.high_hbm, bf16[256,256]{1,0:T(8,128)(2,1)} %constant.5.clone.low_hbm), custom_call_target="tpu_custom_call" | custom-call | tf_op jit(solution)/shard_map/pallas_call | solution.py:280
  43.5 3.3 %shard_map.47 = f32[1,2,256,1024]{3,2,1,0:T(8,128)} custom-call(bf16[4,1024,128]{2,1,0:T(8,128)(2,1)} %bitcast.6), custom_call_target="tpu_custom_call" | custom-call | tf_op jit(solution)/shard_map/pallas_call | solution.py:313

commit v3 on v2

--- a/solution.py
+++ b/solution.py
@@ -21,7 +21,6 @@
     + [(r, k) for k in range(4) for r in (1, 3)]
     + [(0, k) for k in range(1, 4)]
 )
-QUAD_ORDER = (2, 1, 3, 0)
 
 
 def dft_matrix(channels):
@@ -97,7 +96,7 @@
                 ]
     for b in range(2):
         for part in range(2):
-            spec[b, part] = (
+            spec[b * 2 + part] = (
                 inter[b, part].astype(jnp.bfloat16).reshape(NY, NX, NZ, 2, spectra)
             )
 
@@ -157,109 +156,94 @@
             device_id={"chan": c, "pair": p}, device_id_type=MESH,
         )
 
-    def b_copy(b, t):
+    def b_copy(q, t):
         oy, ox = group_ahead(t)
         return remote(
-            spec.at[b, :, oy, ox], near.at[b, :, y, :, x],
-            b_send.at[b, t], b_recv.at[b, t], chan_of(oy, z, ox), pair,
-        )
-
-    def b_arrival(b, t):
+            spec.at[q, oy, ox], near.at[q, y, :, x], b_send.at[q, t], b_recv.at[q, t], chan_of(oy, z, ox), pair
+        )
+
+    def b_arrival(q, t):
         oy, ox = group_ahead(GROUPS - t)
         return remote(
-            spec.at[b, :, oy, ox], near.at[b, :, oy, :, ox],
-            b_send.at[b, t], b_recv.at[b, t], chan_of(oy, z, ox), pair,
-        )
-
-    def a_copy(b, r, k):
+            spec.at[q, oy, ox], near.at[q, oy, :, ox], b_send.at[q, t], b_recv.at[q, t], chan_of(oy, z, ox), pair
+        )
+
+    def a_copy(q, r, k):
         oz = z_ahead(r, k)
         return remote(
-            near.at[b, :, :, oz], out.at[b, :, pair, :, z],
-            a_send.at[b, r * 4 + k], a_recv.at[b, r * 4 + k], chan_of(y, oz, x), pair,
-        )
-
-    def a_arrival(b, r, k):
+            near.at[q, :, oz], out.at[q, pair, :, z],
+            a_send.at[q, r * 4 + k], a_recv.at[q, r * 4 + k], chan_of(y, oz, x), pair,
+        )
+
+    def a_arrival(q, r, k):
         oz = z_behind(r, k)
         return remote(
-            near.at[b, :, :, oz], out.at[b, :, pair, :, oz],
-            a_send.at[b, r * 4 + k], a_recv.at[b, r * 4 + k], chan_of(y, oz, x), pair,
-        )
-
-    def pass_on(b, block, r, target, send, recv):
-        at = pl.ds((quad - r + QUADS) % QUADS * 4, 4)
-        ref = out.at[b, :, block, :, at]
-        return remote(ref, ref, send.at[b, r], recv.at[b, r], chan, target)
-
-    own = [pltpu.make_async_copy(spec.at[b, :, y, x], near.at[b, :, y, :, x], own_sem.at[b]) for b in range(2)]
-    own_z = [pltpu.make_async_copy(near.at[b, :, :, z], out.at[b, :, pair, :, z], own_sem.at[2 + b]) for b in range(2)]
-
-    for b in range(2):
+            near.at[q, :, oz], out.at[q, pair, :, oz],
+            a_send.at[q, r * 4 + k], a_recv.at[q, r * 4 + k], chan_of(y, oz, x), pair,
+        )
+
+    def pass_on(q, block, target, send, recv):
+        ref = out.at[q, block]
+        return remote(ref, ref, send.at[q], recv.at[q], chan, target)
+
+    own = [pltpu.make_async_copy(spec.at[q, y, x], near.at[q, y, :, x], own_sem.at[q]) for q in range(4)]
+    own_z = [pltpu.make_async_copy(near.at[q, :, z], out.at[q, pair, :, z], own_sem.at[4 + q]) for q in range(4)]
+
+    for q in range(4):
         for t in range(1, GROUPS):
-            b_copy(b, t).start()
-        own[b].start()
-    for b in range(2):
-        own[b].wait()
+            b_copy(q, t).start()
+        own[q].start()
+    for q in range(4):
+        own[q].wait()
         for t in range(1, GROUPS):
-            b_arrival(b, t).wait_recv()
+            b_arrival(q, t).wait_recv()
         for r, k in Z_STEPS:
-            a_copy(b, r, k).start()
-        own_z[b].start()
-
-    def gather(b, r):
-        for k in range(4):
-            if r or k:
-                a_arrival(b, r, k).wait_recv()
-        if r == 0:
-            own_z[b].wait()
-        pass_on(b, pair, r, x_mate, x_send, x_recv).start()
-        pass_on(b, pair, r, core_mate, core_send, core_recv).start()
-
-    def forward(b, r):
-        pass_on(b, x_mate, r, x_mate, x_send, x_recv).wait_recv()
-        pass_on(b, x_mate, r, core_mate, on_send, on_recv).start()
-
-    for r in QUAD_ORDER:
-        gather(0, r)
-    for r in QUAD_ORDER:
-        forward(0, r)
-        gather(1, r)
-    for r in QUAD_ORDER:
-        forward(1, r)
+            a_copy(q, r, k).start()
+        own_z[q].start()
+
+    def gather(q):
+        for r, k in Z_STEPS:
+            a_arrival(q, r, k).wait_recv()
+        own_z[q].wait()
+        pass_on(q, pair, x_mate, x_send, x_recv).start()
+        pass_on(q, pair, core_mate, core_send, core_recv).start()
+
+    def forward(q):
+        pass_on(q, x_mate, x_mate, x_send, x_recv).wait_recv()
+        pass_on(q, x_mate, core_mate, on_send, on_recv).start()
+
+    gather(0)
+    for q in range(1, 4):
+        gather(q)
+        forward(q - 1)
+    forward(3)
 
     diagonal = (core_mate + 2) % 4
-    for b in range(2):
-        for r in range(QUADS):
-            pass_on(b, core_mate, r, core_mate, core_send, core_recv).wait_recv()
-            pass_on(b, diagonal, r, core_mate, on_send, on_recv).wait_recv()
-            pass_on(b, pair, r, core_mate, core_send, core_recv).wait_send()
-            pass_on(b, pair, r, x_mate, x_send, x_recv).wait_send()
-            pass_on(b, x_mate, r, core_mate, on_send, on_recv).wait_send()
+    for q in range(4):
+        pass_on(q, core_mate, core_mate, core_send, core_recv).wait_recv()
+        pass_on(q, diagonal, core_mate, on_send, on_recv).wait_recv()
+        pass_on(q, pair, core_mate, core_send, core_recv).wait_send()
+        pass_on(q, pair, x_mate, x_send, x_recv).wait_send()
+        pass_on(q, x_mate, core_mate, on_send, on_recv).wait_send()
         for r, k in Z_STEPS:
-            a_copy(b, r, k).wait_send()
+            a_copy(q, r, k).wait_send()
         for t in range(1, GROUPS):
-            b_copy(b, t).wait_send()
-
-
-def correlate_kernel(scale, everyone, out, held, own, result, in_sem, out_sem):
+            b_copy(q, t).wait_send()
+
+
+def correlate_kernel(scale, everyone, out, result, out_sem):
     tiles, _, block, tile = result.shape
     mine = pl.ds(pl.multiple_of(lax.axis_index("pair") * block, block), block)
-    own_load = pltpu.make_async_copy(everyone.at[:, mine], own, in_sem.at[tiles])
-    own_load.start()
-    loads, stores = [], []
+    rows = [everyone[q, mine, :] for q in range(4)]
+    straight = jnp.concatenate(rows, axis=1)
+    turned = jnp.concatenate([rows[1], -rows[0], rows[3], -rows[2]], axis=1)
+    stores = []
     for g in range(tiles):
         there = pl.ds(g * tile, tile)
-        loads.append(pltpu.make_async_copy(everyone.at[:, there], held.at[g], in_sem.at[g]))
-        stores.append(pltpu.make_async_copy(result.at[g], out.at[0, :, :, there], out_sem.at[g]))
-        loads[g].start()
-    own_load.wait()
-    rows = [own[q] for q in range(4)]
-    straight = jnp.concatenate(rows, axis=1)
-    turned = jnp.concatenate([rows[1], -rows[0], rows[3], -rows[2]], axis=1)
-    for g in range(tiles):
-        loads[g].wait()
-        columns = jnp.concatenate([held[g, q] for q in range(4)], axis=1)
+        columns = jnp.concatenate([everyone[q, there, :] for q in range(4)], axis=1)
         result[g, 0] = nt_dot(straight, columns) * scale
         result[g, 1] = nt_dot(turned, columns) * scale
+        stores.append(pltpu.make_async_copy(result.at[g], out.at[0, :, :, there], out_sem.at[g]))
         stores[g].start()
     for store in stores:
         store.wait()
@@ -276,12 +260,13 @@
     volt = jnp.transpose(volt, (0, 2, 1, 3)).reshape(antennas * batches * samples // half, half)
     high, low = dft_matrix(half)
     hbm = pl.BlockSpec(memory_space=pltpu.HBM)
+    vmem = pl.BlockSpec(memory_space=pltpu.VMEM)
     dma = pltpu.SemaphoreType.DMA
     everyone = pl.pallas_call(
         spread_kernel,
-        out_shape=jax.ShapeDtypeStruct((2, 2, 4, NY, NZ, NX, 2, spectra_len), jnp.bfloat16),
+        out_shape=pltpu.VMEM((4, 4, NY, NZ, NX, 2, spectra_len), jnp.bfloat16),
         in_specs=[hbm] * 4,
-        out_specs=hbm,
+        out_specs=vmem,
         scratch_shapes=[
             pltpu.VMEM(volt.shape, jnp.bfloat16),
             pltpu.VMEM(fir_taps.shape, jnp.float32),
@@ -290,16 +275,16 @@
             pltpu.VMEM(volt.shape, jnp.float32),
             pltpu.VMEM((8 * spectra_len, half), jnp.float32),
             pltpu.VMEM((2, 2, half, 2, spectra_len), jnp.float32),
-            pltpu.VMEM((2, 2, NY, NX, NZ, 2, spectra_len), jnp.bfloat16),
-            pltpu.VMEM((2, 2, NY, NZ, NX, 2, spectra_len), jnp.bfloat16),
+            pltpu.VMEM((4, NY, NX, NZ, 2, spectra_len), jnp.bfloat16),
+            pltpu.VMEM((4, NY, NZ, NX, 2, spectra_len), jnp.bfloat16),
             dma((4,)),
-            dma((4,)),
-            dma((2, GROUPS)),
-            dma((2, GROUPS)),
-            dma((2, NZ)),
-            dma((2, NZ)),
+            dma((8,)),
+            dma((4, GROUPS)),
+            dma((4, GROUPS)),
+            dma((4, NZ)),
+            dma((4, NZ)),
         ]
-        + [dma((2, QUADS))] * 6,
+        + [dma((4,))] * 6,
         compiler_params=pltpu.CompilerParams(
             collective_id=0, has_side_effects=True, vmem_limit_bytes=VMEM_LIMIT
         ),
@@ -313,16 +298,10 @@
     return pl.pallas_call(
         functools.partial(correlate_kernel, scale),
         out_shape=jax.ShapeDtypeStruct((1, 2, block, total), jnp.float32),
-        in_specs=[hbm],
+        in_specs=[vmem],
         out_specs=hbm,
-        scratch_shapes=[
-            pltpu.VMEM((tiles, 4, tile, spectra_len), jnp.bfloat16),
-            pltpu.VMEM((4, block, spectra_len), jnp.bfloat16),
-            pltpu.VMEM((tiles, 2, block, tile), jnp.float32),
-            dma((tiles + 1,)),
-            dma((tiles,)),
-        ],
-        compiler_params=pltpu.CompilerParams(vmem_limit_bytes=VMEM_LIMIT),
+        scratch_shapes=[pltpu.VMEM((tiles, 2, block, tile), jnp.float32), dma((tiles,))],
+        compiler_params=pltpu.CompilerParams(vmem_limit_bytes=8 * 1024 * 1024),
     )(everyone)
 
 

time: 46.9 us -> 44.7 us (0.953)
  Pallas kernels: 46.8 us -> 44.6 us
    pallas_call x1, Pallas kernels: 3.25 us -> 1.68 us  [shards(): pl.pallas_call(functools.partial(correlate_kernel, scale), out_shape=jax....]
    pallas_call x1, Pallas kernels: 43.5 us -> 42.9 us  [shards(): pl.pallas_call(spread_kernel, out_shape=pltpu.VMEM((4, 4, NY, NZ, NX, 2,...]
where the time goes in v3:
time: 44.7 us; the launch traced here: 44.6 us
  Pallas kernels  44.6 us (100%)
    pallas_call x1, Pallas kernels, shards(): pl.pallas_call(spread_kernel, out_shape=pltpu.VMEM((4, 4, NY, NZ, NX, 2,...  42.9 us
    pallas_call x1, Pallas kernels, shards(): pl.pallas_call(functools.partial(correlate_kernel, scale), out_shape=jax....  1.68 us

profile of v3, /device:TPU:1, one launch (start us, length us, event | category | flops | bytes accessed | tf_op | source)
XLA Modules:
  0.0 44.6 jit_solution(9617890907847315021)
XLA Ops:
  0.0 42.9 %shard_map.46 = bf16[4,4,4,16,2,2,128]{6,5,4,3,2,1,0:T(2,128)(2,1)S(1)} custom-call(bf16[1080,128]{1,0:T(8,128)(2,1)} %bitcast.7, f32[8,256]{1,0:T(8,128)} %taps_hbm.1, bf16[256,256]{1,0:T(8,128)(2,1)} %constant.4.clone.high_hbm, bf16[256,256]{1,0:T(8,128)(2,1)} %constant.5.clone.low_hbm), custom_call_target="tpu_custom_call" | custom-call | tf_op jit(solution)/shard_map/pallas_call | solution.py:265
  42.9 1.7 %shard_map.47 = f32[1,2,256,1024]{3,2,1,0:T(8,128)} custom-call(bf16[4,1024,128]{2,1,0:T(8,128)(2,1)S(1)} %bitcast.6), custom_call_target="tpu_custom_call" | custom-call | tf_op jit(solution)/shard_map/pallas_call | solution.py:298

commit v4 on v3

--- a/solution.py
+++ b/solution.py
@@ -14,7 +14,11 @@
 MESH = pl.DeviceIdType.MESH
 NY, NZ, NX = 4, 16, 2
 QUADS = NZ // 4
-GROUPS = NY * NX
+PARTS = 2
+PLANE_STEPS = sorted(
+    ((dy, dx) for dy in range(NY) for dx in range(2 * NX) if dy or dx),
+    key=lambda step: -(min(step[0], NY - step[0]) + min(step[1], 2 * NX - step[1])),
+)
 VMEM_LIMIT = 56 * 1024 * 1024
 Z_STEPS = (
     [(2, k) for k in range(4)]
@@ -25,7 +29,7 @@
 
 def dft_matrix(channels):
     frame = 2 * channels
-    part, y, x, z = np.meshgrid(np.arange(2), np.arange(NY), np.arange(NX), np.arange(NZ), indexing="ij")
+    part, z, y, x = np.meshgrid(np.arange(2), np.arange(NZ), np.arange(NY), np.arange(NX), indexing="ij")
     freq = ((y * NZ + z) * NX + x).reshape(-1)
     part = part.reshape(-1)
     phases = freq[:, None] * np.arange(frame)[None, :] % frame
@@ -97,14 +101,14 @@
     for b in range(2):
         for part in range(2):
             spec[b * 2 + part] = (
-                inter[b, part].astype(jnp.bfloat16).reshape(NY, NX, NZ, 2, spectra)
+                inter[b, part].astype(jnp.bfloat16).reshape(NZ, NY, NX, 2, spectra)
             )
 
 
 def spread_kernel(
-    volt_hbm, taps_hbm, high_hbm, low_hbm, out,
+    parts, volt_hbm, taps_hbm, high_hbm, low_hbm, out,
     volt, taps, high, low, wide, filt, inter, spec, near,
-    load_sem, own_sem, b_send, b_recv, a_send, a_recv, core_send, core_recv, x_send, x_recv, on_send, on_recv,
+    load_sem, own_sem, z_send, z_recv, plane_send, plane_recv, core_send, core_recv,
 ):
     loads = [
         pltpu.make_async_copy(source, target, load_sem.at[i])
@@ -114,17 +118,12 @@
         load.start()
 
     chan, pair = lax.axis_index("chan"), lax.axis_index("pair")
-    y, z, x = chan // (NZ * NX), (chan // NX) % NZ, chan % NX
+    y, z, x_hi = chan // (NZ * NX), (chan // NX) % NZ, chan % NX
+    x = x_hi * 2 + pair // 2
+    core = pair % 2
     quad, place = z // 4, z % 4
-    core_mate = pair + 1 - 2 * (pair % 2)
+    core_mate = pair + 1 - 2 * core
     x_mate = (pair + 2) % 4
-
-    def chan_of(y, z, x):
-        return (y * NZ + z) * NX + x
-
-    def group_ahead(t):
-        d = (y * NX + x + t) % GROUPS
-        return d // NX, d % NX
 
     def z_ahead(r, k):
         return (quad + r) % QUADS * 4 + (place + k) % 4
@@ -132,103 +131,118 @@
     def z_behind(r, k):
         return (quad - r + QUADS) % QUADS * 4 + (place - k + 4) % 4
 
+    def along_z(oz):
+        return {"chan": (y * NZ + oz) * NX + x_hi, "pair": pair}
+
+    def in_plane(oy, ox):
+        return {"chan": (oy * NZ + z) * NX + ox // 2, "pair": ox % 2 * 2 + core}
+
     barrier = pltpu.get_barrier_semaphore()
 
-    def greet(c, p):
-        pl.semaphore_signal(barrier, inc=1, device_id={"chan": c, "pair": p}, device_id_type=MESH)
+    def greet(device):
+        pl.semaphore_signal(barrier, inc=1, device_id=device, device_id_type=MESH)
 
     for r, k in Z_STEPS:
-        greet(chan_of(y, z_ahead(r, k), x), pair)
-    for t in range(1, GROUPS):
-        oy, ox = group_ahead(t)
-        greet(chan_of(oy, z, ox), pair)
-    greet(chan, x_mate)
-    greet(chan, core_mate)
+        greet(along_z(z_ahead(r, k)))
+    for dy, dx in PLANE_STEPS:
+        greet(in_plane((y + dy) % NY, (x + dx) % (2 * NX)))
+    greet({"chan": chan, "pair": core_mate})
 
     for load in loads:
         load.wait()
     channelize(volt, taps, high, low, spec, wide, filt, inter)
-    pl.semaphore_wait(barrier, len(Z_STEPS) + GROUPS - 1 + 2)
-
-    def remote(source, target, send, recv, c, p):
+    pl.semaphore_wait(barrier, len(Z_STEPS) + len(PLANE_STEPS) + 1)
+
+    def remote(source, target, send, recv, device):
         return pltpu.make_async_remote_copy(
             src_ref=source, dst_ref=target, send_sem=send, recv_sem=recv,
-            device_id={"chan": c, "pair": p}, device_id_type=MESH,
-        )
-
-    def b_copy(q, t):
-        oy, ox = group_ahead(t)
-        return remote(
-            spec.at[q, oy, ox], near.at[q, y, :, x], b_send.at[q, t], b_recv.at[q, t], chan_of(oy, z, ox), pair
-        )
-
-    def b_arrival(q, t):
-        oy, ox = group_ahead(GROUPS - t)
-        return remote(
-            spec.at[q, oy, ox], near.at[q, oy, :, ox], b_send.at[q, t], b_recv.at[q, t], chan_of(oy, z, ox), pair
-        )
-
-    def a_copy(q, r, k):
+            device_id=device, device_id_type=MESH,
+        )
+
+    size = 4 // parts
+
+    def rows(p):
+        return pl.ds(p * size, size)
+
+    def z_copy(p, r, k):
         oz = z_ahead(r, k)
         return remote(
-            near.at[q, :, oz], out.at[q, pair, :, z],
-            a_send.at[q, r * 4 + k], a_recv.at[q, r * 4 + k], chan_of(y, oz, x), pair,
-        )
-
-    def a_arrival(q, r, k):
+            spec.at[rows(p), oz], near.at[rows(p), :, :, z],
+            z_send.at[p, r * 4 + k], z_recv.at[p, r * 4 + k], along_z(oz),
+        )
+
+    def z_arrival(p, r, k):
         oz = z_behind(r, k)
         return remote(
-            near.at[q, :, oz], out.at[q, pair, :, oz],
-            a_send.at[q, r * 4 + k], a_recv.at[q, r * 4 + k], chan_of(y, oz, x), pair,
-        )
-
-    def pass_on(q, block, target, send, recv):
-        ref = out.at[q, block]
-        return remote(ref, ref, send.at[q], recv.at[q], chan, target)
-
-    own = [pltpu.make_async_copy(spec.at[q, y, x], near.at[q, y, :, x], own_sem.at[q]) for q in range(4)]
-    own_z = [pltpu.make_async_copy(near.at[q, :, z], out.at[q, pair, :, z], own_sem.at[4 + q]) for q in range(4)]
-
-    for q in range(4):
-        for t in range(1, GROUPS):
-            b_copy(q, t).start()
-        own[q].start()
-    for q in range(4):
-        own[q].wait()
-        for t in range(1, GROUPS):
-            b_arrival(q, t).wait_recv()
+            spec.at[rows(p), oz], near.at[rows(p), :, :, oz],
+            z_send.at[p, r * 4 + k], z_recv.at[p, r * 4 + k], along_z(oz),
+        )
+
+    def plane_copy(p, dy, dx):
+        oy, ox = (y + dy) % NY, (x + dx) % (2 * NX)
+        return remote(
+            near.at[rows(p), oy, ox // 2], out.at[rows(p), pair, y, :, x_hi],
+            plane_send.at[p, dy * 4 + dx], plane_recv.at[p, dy * 4 + dx], in_plane(oy, ox),
+        )
+
+    def plane_arrival(p, dy, dx):
+        oy, ox = (y - dy + NY) % NY, (x - dx + 2 * NX) % (2 * NX)
+        return remote(
+            near.at[rows(p), oy, ox // 2], out.at[rows(p), ox % 2 * 2 + core, oy, :, ox // 2],
+            plane_send.at[p, dy * 4 + dx], plane_recv.at[p, dy * 4 + dx], in_plane(oy, ox),
+        )
+
+    def core_copy(p, block, odd):
+        ref = out.at[rows(p), block]
+        return remote(
+            ref, ref, core_send.at[p, odd], core_recv.at[p, odd], {"chan": chan, "pair": core_mate}
+        )
+
+    own_z = [
+        pltpu.make_async_copy(spec.at[rows(p), z], near.at[rows(p), :, :, z], own_sem.at[p]) for p in range(parts)
+    ]
+    own = [
+        pltpu.make_async_copy(near.at[rows(p), y, x_hi], out.at[rows(p), pair, y, :, x_hi], own_sem.at[parts + p])
+        for p in range(parts)
+    ]
+
+    for p in range(parts):
         for r, k in Z_STEPS:
-            a_copy(q, r, k).start()
-        own_z[q].start()
-
-    def gather(q):
+            z_copy(p, r, k).start()
+        own_z[p].start()
+
+    def spread(p):
+        own_z[p].wait()
         for r, k in Z_STEPS:
-            a_arrival(q, r, k).wait_recv()
-        own_z[q].wait()
-        pass_on(q, pair, x_mate, x_send, x_recv).start()
-        pass_on(q, pair, core_mate, core_send, core_recv).start()
-
-    def forward(q):
-        pass_on(q, x_mate, x_mate, x_send, x_recv).wait_recv()
-        pass_on(q, x_mate, core_mate, on_send, on_recv).start()
-
-    gather(0)
-    for q in range(1, 4):
-        gather(q)
-        forward(q - 1)
-    forward(3)
-
-    diagonal = (core_mate + 2) % 4
-    for q in range(4):
-        pass_on(q, core_mate, core_mate, core_send, core_recv).wait_recv()
-        pass_on(q, diagonal, core_mate, on_send, on_recv).wait_recv()
-        pass_on(q, pair, core_mate, core_send, core_recv).wait_send()
-        pass_on(q, pair, x_mate, x_send, x_recv).wait_send()
-        pass_on(q, x_mate, core_mate, on_send, on_recv).wait_send()
+            z_arrival(p, r, k).wait_recv()
+        for dy, dx in PLANE_STEPS:
+            plane_copy(p, dy, dx).start()
+        own[p].start()
+
+    def share(p):
+        for odd, block in ((1, x_mate), (0, pair)):
+            if not odd:
+                own[p].wait()
+            for dy, dx in PLANE_STEPS:
+                if dx % 2 == odd:
+                    plane_arrival(p, dy, dx).wait_recv()
+            core_copy(p, block, odd).start()
+
+    spread(0)
+    for p in range(1, parts):
+        spread(p)
+        share(p - 1)
+    share(parts - 1)
+
+    for p in range(parts):
+        core_copy(p, (x_mate + 1 - 2 * core), 1).wait_recv()
+        core_copy(p, core_mate, 0).wait_recv()
+        core_copy(p, x_mate, 1).wait_send()
+        core_copy(p, pair, 0).wait_send()
         for r, k in Z_STEPS:
-            a_copy(q, r, k).wait_send()
-        for t in range(1, GROUPS):
-            b_copy(q, t).wait_send()
+            z_copy(p, r, k).wait_send()
+        for dy, dx in PLANE_STEPS:
+            plane_copy(p, dy, dx).wait_send()
 
 
 def correlate_kernel(scale, everyone, out, result, out_sem):
@@ -263,7 +277,7 @@
     vmem = pl.BlockSpec(memory_space=pltpu.VMEM)
     dma = pltpu.SemaphoreType.DMA
     everyone = pl.pallas_call(
-        spread_kernel,
+        functools.partial(spread_kernel, PARTS),
         out_shape=pltpu.VMEM((4, 4, NY, NZ, NX, 2, spectra_len), jnp.bfloat16),
         in_specs=[hbm] * 4,
         out_specs=vmem,
@@ -275,16 +289,17 @@
             pltpu.VMEM(volt.shape, jnp.float32),
             pltpu.VMEM((8 * spectra_len, half), jnp.float32),
             pltpu.VMEM((2, 2, half, 2, spectra_len), jnp.float32),
+            pltpu.VMEM((4, NZ, NY, NX, 2, spectra_len), jnp.bfloat16),
             pltpu.VMEM((4, NY, NX, NZ, 2, spectra_len), jnp.bfloat16),
-            pltpu.VMEM((4, NY, NZ, NX, 2, spectra_len), jnp.bfloat16),
             dma((4,)),
-            dma((8,)),
-            dma((4, GROUPS)),
-            dma((4, GROUPS)),
-            dma((4, NZ)),
-            dma((4, NZ)),
-        ]
-        + [dma((4,))] * 6,
+            dma((2 * PARTS,)),
+            dma((PARTS, NZ)),
+            dma((PARTS, NZ)),
+            dma((PARTS, NY * 2 * NX)),
+            dma((PARTS, NY * 2 * NX)),
+            dma((PARTS, 2)),
+            dma((PARTS, 2)),
+        ],
         compiler_params=pltpu.CompilerParams(
             collective_id=0, has_side_effects=True, vmem_limit_bytes=VMEM_LIMIT
         ),

time: 44.7 us -> 41.6 us (0.931)
  Pallas kernels: 44.6 us -> 41.5 us
    pallas_call x1, Pallas kernels: 42.9 us -> 39.8 us  [shards(): pl.pallas_call(functools.partial(spread_kernel, PARTS), out_shape=pltpu.V...]
where the time goes in v4:
time: 41.6 us; the launch traced here: 41.5 us
  Pallas kernels  41.5 us (100%)
    pallas_call x1, Pallas kernels, shards(): pl.pallas_call(functools.partial(spread_kernel, PARTS), out_shape=pltpu.V...  39.8 us
    pallas_call x1, Pallas kernels, shards(): pl.pallas_call(functools.partial(correlate_kernel, scale), out_shape=jax....  1.68 us

profile of v4, /device:TPU:1, one launch (start us, length us, event | category | flops | bytes accessed | tf_op | source)
XLA Modules:
  0.0 41.5 jit_solution(15094308622673073170)
XLA Ops:
  0.0 39.8 %shard_map.46 = bf16[4,4,4,16,2,2,128]{6,5,4,3,2,1,0:T(2,128)(2,1)S(1)} custom-call(bf16[1080,128]{1,0:T(8,128)(2,1)} %bitcast.7, f32[8,256]{1,0:T(8,128)} %taps_hbm.1, bf16[256,256]{1,0:T(8,128)(2,1)} %constant.4.clone.high_hbm, bf16[256,256]{1,0:T(8,128)(2,1)} %constant.5.clone.low_hbm), custom_call_target="tpu_custom_call" | custom-call | tf_op jit(solution)/shard_map/pallas_call | solution.py:279
  39.8 1.7 %shard_map.47 = f32[1,2,256,1024]{3,2,1,0:T(8,128)} custom-call(bf16[4,1024,128]{2,1,0:T(8,128)(2,1)S(1)} %bitcast.6), custom_call_target="tpu_custom_call" | custom-call | tf_op jit(solution)/shard_map/pallas_call | solution.py:313

commit v5 on v4

--- a/solution.py
+++ b/solution.py
@@ -13,18 +13,13 @@
 
 MESH = pl.DeviceIdType.MESH
 NY, NZ, NX = 4, 16, 2
-QUADS = NZ // 4
+Z_ORDER = (0, 4, 1, 5, 2, 6, 3, 7, 12, 8, 13, 9, 14, 10, 15, 11)
 PARTS = 2
 PLANE_STEPS = sorted(
     ((dy, dx) for dy in range(NY) for dx in range(2 * NX) if dy or dx),
     key=lambda step: -(min(step[0], NY - step[0]) + min(step[1], 2 * NX - step[1])),
 )
 VMEM_LIMIT = 56 * 1024 * 1024
-Z_STEPS = (
-    [(2, k) for k in range(4)]
-    + [(r, k) for k in range(4) for r in (1, 3)]
-    + [(0, k) for k in range(1, 4)]
-)
 
 
 def dft_matrix(channels):
@@ -121,15 +116,12 @@
     y, z, x_hi = chan // (NZ * NX), (chan // NX) % NZ, chan % NX
     x = x_hi * 2 + pair // 2
     core = pair % 2
-    quad, place = z // 4, z % 4
     core_mate = pair + 1 - 2 * core
     x_mate = (pair + 2) % 4
 
-    def z_ahead(r, k):
-        return (quad + r) % QUADS * 4 + (place + k) % 4
-
-    def z_behind(r, k):
-        return (quad - r + QUADS) % QUADS * 4 + (place - k + 4) % 4
+    def others(steps, each):
+        for oz in steps:
+            pl.when(z != oz)(functools.partial(each, oz))
 
     def along_z(oz):
         return {"chan": (y * NZ + oz) * NX + x_hi, "pair": pair}
@@ -142,8 +134,8 @@
     def greet(device):
         pl.semaphore_signal(barrier, inc=1, device_id=device, device_id_type=MESH)
 
-    for r, k in Z_STEPS:
-        greet(along_z(z_ahead(r, k)))
+    for step in range(1, NZ):
+        greet(along_z((z + (NZ // 2 + step // 2 if step % 2 else NZ // 2 - step // 2)) % NZ))
     for dy, dx in PLANE_STEPS:
         greet(in_plane((y + dy) % NY, (x + dx) % (2 * NX)))
     greet({"chan": chan, "pair": core_mate})
@@ -151,7 +143,7 @@
     for load in loads:
         load.wait()
     channelize(volt, taps, high, low, spec, wide, filt, inter)
-    pl.semaphore_wait(barrier, len(Z_STEPS) + len(PLANE_STEPS) + 1)
+    pl.semaphore_wait(barrier, NZ - 1 + len(PLANE_STEPS) + 1)
 
     def remote(source, target, send, recv, device):
         return pltpu.make_async_remote_copy(
@@ -164,18 +156,14 @@
     def rows(p):
         return pl.ds(p * size, size)
 
-    def z_copy(p, r, k):
-        oz = z_ahead(r, k)
-        return remote(
-            spec.at[rows(p), oz], near.at[rows(p), :, :, z],
-            z_send.at[p, r * 4 + k], z_recv.at[p, r * 4 + k], along_z(oz),
-        )
-
-    def z_arrival(p, r, k):
-        oz = z_behind(r, k)
-        return remote(
-            spec.at[rows(p), oz], near.at[rows(p), :, :, oz],
-            z_send.at[p, r * 4 + k], z_recv.at[p, r * 4 + k], along_z(oz),
+    def z_copy(p, oz):
+        return remote(
+            spec.at[rows(p), oz], near.at[rows(p), :, :, z], z_send.at[p, oz], z_recv.at[p, z], along_z(oz)
+        )
+
+    def z_arrival(p, oz):
+        return remote(
+            spec.at[rows(p), oz], near.at[rows(p), :, :, oz], z_send.at[p, oz], z_recv.at[p, oz], along_z(oz)
         )
 
     def plane_copy(p, dy, dx):
@@ -206,15 +194,17 @@
         for p in range(parts)
     ]
 
+    def send(oz):
+        for p in range(parts):
+            z_copy(p, oz).start()
+
     for p in range(parts):
-        for r, k in Z_STEPS:
-            z_copy(p, r, k).start()
         own_z[p].start()
+    others(Z_ORDER, send)
 
     def spread(p):
         own_z[p].wait()
-        for r, k in Z_STEPS:
-            z_arrival(p, r, k).wait_recv()
+        others(range(NZ), lambda oz: z_arrival(p, oz).wait_recv())
         for dy, dx in PLANE_STEPS:
             plane_copy(p, dy, dx).start()
         own[p].start()
@@ -239,8 +229,7 @@
         core_copy(p, core_mate, 0).wait_recv()
         core_copy(p, x_mate, 1).wait_send()
         core_copy(p, pair, 0).wait_send()
-        for r, k in Z_STEPS:
-            z_copy(p, r, k).wait_send()
+        others(range(NZ), lambda oz: z_copy(p, oz).wait_send())
         for dy, dx in PLANE_STEPS:
             plane_copy(p, dy, dx).wait_send()
 

time: 41.6 us -> 41.1 us (0.988)
  the two profiles are of different devices: /device:TPU:1 before, /device:TPU:97 now
where the time goes in v5:
time: 41.1 us; the launch traced here: 40.9 us
  Pallas kernels  40.9 us (100%)
    pallas_call x1, Pallas kernels, shards(): pl.pallas_call(functools.partial(spread_kernel, PARTS), out_shape=pltpu.V...  39.2 us
    pallas_call x1, Pallas kernels, shards(): pl.pallas_call(functools.partial(correlate_kernel, scale), out_shape=jax....  1.68 us

profile of v5, /device:TPU:97, one launch (start us, length us, event | category | flops | bytes accessed | tf_op | source)
XLA Modules:
  0.0 40.9 jit_solution(14966746255686664261)
XLA Ops:
  0.0 39.2 %shard_map.46 = bf16[4,4,4,16,2,2,128]{6,5,4,3,2,1,0:T(2,128)(2,1)S(1)} custom-call(bf16[1080,128]{1,0:T(8,128)(2,1)} %bitcast.7, f32[8,256]{1,0:T(8,128)} %taps_hbm.1, bf16[256,256]{1,0:T(8,128)(2,1)} %constant.4.clone.high_hbm, bf16[256,256]{1,0:T(8,128)(2,1)} %constant.5.clone.low_hbm), custom_call_target="tpu_custom_call" | custom-call | tf_op jit(solution)/shard_map/pallas_call | solution.py:268
  39.3 1.7 %shard_map.47 = f32[1,2,256,1024]{3,2,1,0:T(8,128)} custom-call(bf16[4,1024,128]{2,1,0:T(8,128)(2,1)S(1)} %bitcast.6), custom_call_target="tpu_custom_call" | custom-call | tf_op jit(solution)/shard_map/pallas_call | solution.py:302

commit v6 on v5

--- a/solution.py
+++ b/solution.py
@@ -13,7 +13,23 @@
 
 MESH = pl.DeviceIdType.MESH
 NY, NZ, NX = 4, 16, 2
-Z_ORDER = (0, 4, 1, 5, 2, 6, 3, 7, 12, 8, 13, 9, 14, 10, 15, 11)
+STARTS = (0.0, 0.7, 1.6, 2.5, 4.1, 5.0, 5.9, 6.9, 8.4, 8.4, 8.4, 8.4, 7.8, 7.8, 7.8, 7.8)
+DUE, FAR = 1.0, 0.65
+EARLY = 7
+RELAY = {oz: EARLY - 1 if oz < (EARLY + NZ + 1) // 2 else 0 for oz in range(EARLY, NZ)}
+
+
+def hops(a, b):
+    return min((a - b) % NZ, (b - a) % NZ)
+
+
+Z_TABLE = [
+    sorted(
+        (o for o in range(NZ) if o != z),
+        key=lambda o: (z >= EARLY and o >= EARLY, DUE * STARTS[o] - FAR * hops(z, o), (o - z) % NZ),
+    )
+    for z in range(NZ)
+]
 PARTS = 2
 PLANE_STEPS = sorted(
     ((dy, dx) for dy in range(NY) for dx in range(2 * NX) if dy or dx),
@@ -103,7 +119,7 @@
 def spread_kernel(
     parts, volt_hbm, taps_hbm, high_hbm, low_hbm, out,
     volt, taps, high, low, wide, filt, inter, spec, near,
-    load_sem, own_sem, z_send, z_recv, plane_send, plane_recv, core_send, core_recv,
+    late_sem, load_sem, own_sem, z_send, z_recv, plane_send, plane_recv, core_send, core_recv,
 ):
     loads = [
         pltpu.make_async_copy(source, target, load_sem.at[i])
@@ -135,7 +151,8 @@
         pl.semaphore_signal(barrier, inc=1, device_id=device, device_id_type=MESH)
 
     for step in range(1, NZ):
-        greet(along_z((z + (NZ // 2 + step // 2 if step % 2 else NZ // 2 - step // 2)) % NZ))
+        oz = (z + (NZ // 2 + step // 2 if step % 2 else NZ // 2 - step // 2)) % NZ
+        pl.when(jnp.logical_or(z < EARLY, oz < EARLY))(functools.partial(greet, along_z(oz)))
     for dy, dx in PLANE_STEPS:
         greet(in_plane((y + dy) % NY, (x + dx) % (2 * NX)))
     greet({"chan": chan, "pair": core_mate})
@@ -143,7 +160,23 @@
     for load in loads:
         load.wait()
     channelize(volt, taps, high, low, spec, wide, filt, inter)
-    pl.semaphore_wait(barrier, NZ - 1 + len(PLANE_STEPS) + 1)
+    mates = len(PLANE_STEPS) + 1
+
+    @pl.when(z >= EARLY)
+    def _():
+        pl.semaphore_wait(barrier, EARLY + mates)
+
+    @pl.when(z < EARLY)
+    def _():
+        pl.semaphore_wait(barrier, NZ - 1 + mates)
+
+    for relay in sorted(set(RELAY.values())):
+
+        @pl.when(z == relay)
+        def _():
+            for oz in RELAY:
+                if RELAY[oz] == relay:
+                    pl.semaphore_signal(late_sem, inc=1, device_id=along_z(oz), device_id_type=MESH)
 
     def remote(source, target, send, recv, device):
         return pltpu.make_async_remote_copy(
@@ -200,7 +233,17 @@
 
     for p in range(parts):
         own_z[p].start()
-    others(Z_ORDER, send)
+    for step in range(NZ - 1):
+        if step == EARLY:
+
+            @pl.when(z >= EARLY)
+            def _():
+                pl.semaphore_wait(late_sem, 1)
+
+        target = Z_TABLE[0][step]
+        for oz in range(1, NZ):
+            target = jnp.where(z == oz, Z_TABLE[oz][step], target)
+        send(target)
 
     def spread(p):
         own_z[p].wait()
@@ -280,6 +323,7 @@
             pltpu.VMEM((2, 2, half, 2, spectra_len), jnp.float32),
             pltpu.VMEM((4, NZ, NY, NX, 2, spectra_len), jnp.bfloat16),
             pltpu.VMEM((4, NY, NX, NZ, 2, spectra_len), jnp.bfloat16),
+            pltpu.SemaphoreType.REGULAR,
             dma((4,)),
             dma((2 * PARTS,)),
             dma((PARTS, NZ)),

time: 41.1 us -> 38.1 us (0.927)
  Pallas kernels: 40.9 us -> 38 us
    pallas_call x1, Pallas kernels: 39.2 us -> 36.3 us  [shards(): pl.pallas_call(functools.partial(spread_kernel, PARTS), out_shape=pltpu.V...]
where the time goes in v6:
time: 38.1 us; the launch traced here: 38 us
  Pallas kernels  38 us (100%)
    pallas_call x1, Pallas kernels, shards(): pl.pallas_call(functools.partial(spread_kernel, PARTS), out_shape=pltpu.V...  36.3 us
    pallas_call x1, Pallas kernels, shards(): pl.pallas_call(functools.partial(correlate_kernel, scale), out_shape=jax....  1.68 us

profile of v6, /device:TPU:97, one launch (start us, length us, event | category | flops | bytes accessed | tf_op | source)
XLA Modules:
  0.0 38.0 jit_solution(5764860479467522384)
XLA Ops:
  0.0 36.3 %shard_map.46 = bf16[4,4,4,16,2,2,128]{6,5,4,3,2,1,0:T(2,128)(2,1)S(1)} custom-call(bf16[1080,128]{1,0:T(8,128)(2,1)} %bitcast.7, f32[8,256]{1,0:T(8,128)} %taps_hbm.1, bf16[256,256]{1,0:T(8,128)(2,1)} %constant.4.clone.high_hbm, bf16[256,256]{1,0:T(8,128)(2,1)} %constant.5.clone.low_hbm), custom_call_target="tpu_custom_call" | custom-call | tf_op jit(solution)/shard_map/pallas_call | solution.py:311
  36.3 1.7 %shard_map.47 = f32[1,2,256,1024]{3,2,1,0:T(8,128)} custom-call(bf16[4,1024,128]{2,1,0:T(8,128)(2,1)S(1)} %bitcast.6), custom_call_target="tpu_custom_call" | custom-call | tf_op jit(solution)/shard_map/pallas_call | solution.py:346

commit v7 on v6

--- a/solution.py
+++ b/solution.py
@@ -15,7 +15,8 @@
 NY, NZ, NX = 4, 16, 2
 STARTS = (0.0, 0.7, 1.6, 2.5, 4.1, 5.0, 5.9, 6.9, 8.4, 8.4, 8.4, 8.4, 7.8, 7.8, 7.8, 7.8)
 DUE, FAR = 1.0, 0.65
-EARLY = 7
+EARLY = 6
+CORE_ORDER = (2, 1, 3, 0)
 RELAY = {oz: EARLY - 1 if oz < (EARLY + NZ + 1) // 2 else 0 for oz in range(EARLY, NZ)}
 
 
@@ -30,7 +31,7 @@
     )
     for z in range(NZ)
 ]
-PARTS = 2
+PARTS = 1
 PLANE_STEPS = sorted(
     ((dy, dx) for dy in range(NY) for dx in range(2 * NX) if dy or dx),
     key=lambda step: -(min(step[0], NY - step[0]) + min(step[1], 2 * NX - step[1])),
@@ -213,10 +214,11 @@
             plane_send.at[p, dy * 4 + dx], plane_recv.at[p, dy * 4 + dx], in_plane(oy, ox),
         )
 
-    def core_copy(p, block, odd):
-        ref = out.at[rows(p), block]
-        return remote(
-            ref, ref, core_send.at[p, odd], core_recv.at[p, odd], {"chan": chan, "pair": core_mate}
+    def core_copy(p, block, odd, dy):
+        ref = out.at[rows(p), block, (y - dy + NY) % NY]
+        at = odd * NY + dy
+        return remote(
+            ref, ref, core_send.at[p, at], core_recv.at[p, at], {"chan": chan, "pair": core_mate}
         )
 
     own_z = [
@@ -227,23 +229,27 @@
         for p in range(parts)
     ]
 
-    def send(oz):
-        for p in range(parts):
-            z_copy(p, oz).start()
-
     for p in range(parts):
         own_z[p].start()
-    for step in range(NZ - 1):
-        if step == EARLY:
-
-            @pl.when(z >= EARLY)
-            def _():
-                pl.semaphore_wait(late_sem, 1)
-
-        target = Z_TABLE[0][step]
-        for oz in range(1, NZ):
-            target = jnp.where(z == oz, Z_TABLE[oz][step], target)
-        send(target)
+    def target(step):
+        oz = Z_TABLE[0][step]
+        for own_plane in range(1, NZ):
+            oz = jnp.where(z == own_plane, Z_TABLE[own_plane][step], oz)
+        return oz
+
+    early_steps = [target(step) for step in range(EARLY)]
+    late_steps = [target(step) for step in range(EARLY, NZ - 1)]
+    for p in range(parts):
+        for oz in early_steps:
+            z_copy(p, oz).start()
+
+    @pl.when(z >= EARLY)
+    def _():
+        pl.semaphore_wait(late_sem, 1)
+
+    for p in range(parts):
+        for oz in late_steps:
+            z_copy(p, oz).start()
 
     def spread(p):
         own_z[p].wait()
@@ -253,13 +259,14 @@
         own[p].start()
 
     def share(p):
-        for odd, block in ((1, x_mate), (0, pair)):
-            if not odd:
-                own[p].wait()
-            for dy, dx in PLANE_STEPS:
-                if dx % 2 == odd:
-                    plane_arrival(p, dy, dx).wait_recv()
-            core_copy(p, block, odd).start()
+        for dy in CORE_ORDER:
+            for odd, block in ((0, pair), (1, x_mate)):
+                if not odd and not dy:
+                    own[p].wait()
+                for step in PLANE_STEPS:
+                    if step[0] == dy and step[1] % 2 == odd:
+                        plane_arrival(p, *step).wait_recv()
+                core_copy(p, block, odd, dy).start()
 
     spread(0)
     for p in range(1, parts):
@@ -268,10 +275,11 @@
     share(parts - 1)
 
     for p in range(parts):
-        core_copy(p, (x_mate + 1 - 2 * core), 1).wait_recv()
-        core_copy(p, core_mate, 0).wait_recv()
-        core_copy(p, x_mate, 1).wait_send()
-        core_copy(p, pair, 0).wait_send()
+        for dy in range(NY):
+            core_copy(p, x_mate + 1 - 2 * core, 1, dy).wait_recv()
+            core_copy(p, core_mate, 0, dy).wait_recv()
+            core_copy(p, x_mate, 1, dy).wait_send()
+            core_copy(p, pair, 0, dy).wait_send()
         others(range(NZ), lambda oz: z_copy(p, oz).wait_send())
         for dy, dx in PLANE_STEPS:
             plane_copy(p, dy, dx).wait_send()
@@ -330,8 +338,8 @@
             dma((PARTS, NZ)),
             dma((PARTS, NY * 2 * NX)),
             dma((PARTS, NY * 2 * NX)),
-            dma((PARTS, 2)),
-            dma((PARTS, 2)),
+            dma((PARTS, 2 * NY)),
+            dma((PARTS, 2 * NY)),
         ],
         compiler_params=pltpu.CompilerParams(
             collective_id=0, has_side_effects=True, vmem_limit_bytes=VMEM_LIMIT

time: 38.1 us -> 36.8 us (0.966)
  the two profiles are of different devices: /device:TPU:97 before, /device:TPU:1 now
where the time goes in v7:
time: 36.8 us; the launch traced here: 36.1 us
  Pallas kernels  36.1 us (98%)
    pallas_call x1, Pallas kernels, shards(): pl.pallas_call(functools.partial(spread_kernel, PARTS), out_shape=pltpu.V...  34.4 us
    pallas_call x1, Pallas kernels, shards(): pl.pallas_call(functools.partial(correlate_kernel, scale), out_shape=jax....  1.68 us

profile of v7, /device:TPU:1, one launch (start us, length us, event | category | flops | bytes accessed | tf_op | source)
XLA Modules:
  0.0 36.1 jit_solution(13808243864204425388)
XLA Ops:
  0.0 34.4 %shard_map.46 = bf16[4,4,4,16,2,2,128]{6,5,4,3,2,1,0:T(2,128)(2,1)S(1)} custom-call(bf16[1080,128]{1,0:T(8,128)(2,1)} %bitcast.7, f32[8,256]{1,0:T(8,128)} %taps_hbm.1, bf16[256,256]{1,0:T(8,128)(2,1)} %constant.4.clone.high_hbm, bf16[256,256]{1,0:T(8,128)(2,1)} %constant.5.clone.low_hbm), custom_call_target="tpu_custom_call" | custom-call | tf_op jit(solution)/shard_map/pallas_call | solution.py:319
  34.4 1.7 %shard_map.47 = f32[1,2,256,1024]{3,2,1,0:T(8,128)} custom-call(bf16[4,1024,128]{2,1,0:T(8,128)(2,1)S(1)} %bitcast.6), custom_call_target="tpu_custom_call" | custom-call | tf_op jit(solution)/shard_map/pallas_call | solution.py:354

commit v8 on v7

--- a/solution.py
+++ b/solution.py
@@ -295,10 +295,11 @@
     for g in range(tiles):
         there = pl.ds(g * tile, tile)
         columns = jnp.concatenate([everyone[q, there, :] for q in range(4)], axis=1)
-        result[g, 0] = nt_dot(straight, columns) * scale
-        result[g, 1] = nt_dot(turned, columns) * scale
-        stores.append(pltpu.make_async_copy(result.at[g], out.at[0, :, :, there], out_sem.at[g]))
-        stores[g].start()
+        for part, side in enumerate((straight, turned)):
+            result[g, part] = nt_dot(side, columns) * scale
+            store = pltpu.make_async_copy(result.at[g, part], out.at[0, part, :, there], out_sem.at[g, part])
+            store.start()
+            stores.append(store)
     for store in stores:
         store.wait()
 
@@ -356,7 +357,7 @@
         out_shape=jax.ShapeDtypeStruct((1, 2, block, total), jnp.float32),
         in_specs=[vmem],
         out_specs=hbm,
-        scratch_shapes=[pltpu.VMEM((tiles, 2, block, tile), jnp.float32), dma((tiles,))],
+        scratch_shapes=[pltpu.VMEM((tiles, 2, block, tile), jnp.float32), dma((tiles, 2))],
         compiler_params=pltpu.CompilerParams(vmem_limit_bytes=8 * 1024 * 1024),
     )(everyone)
 

time: 36.8 us -> 36.9 us (level)
  no operation moved by 1% of the time
where the time goes in v8:
time: 36.9 us; the launch traced here: 36.2 us
  Pallas kernels  36.1 us (98%)
    pallas_call x1, Pallas kernels, shards(): pl.pallas_call(functools.partial(spread_kernel, PARTS), out_shape=pltpu.V...  34.4 us
    pallas_call x1, Pallas kernels, shards(): pl.pallas_call(functools.partial(correlate_kernel, scale), out_shape=jax....  1.71 us

profile of v8, /device:TPU:1, one launch (start us, length us, event | category | flops | bytes accessed | tf_op | source)
XLA Modules:
  0.0 36.2 jit_solution(13216655688424153421)
XLA Ops:
  0.0 34.4 %shard_map.46 = bf16[4,4,4,16,2,2,128]{6,5,4,3,2,1,0:T(2,128)(2,1)S(1)} custom-call(bf16[1080,128]{1,0:T(8,128)(2,1)} %bitcast.7, f32[8,256]{1,0:T(8,128)} %taps_hbm.1, bf16[256,256]{1,0:T(8,128)(2,1)} %constant.4.clone.high_hbm, bf16[256,256]{1,0:T(8,128)(2,1)} %constant.5.clone.low_hbm), custom_call_target="tpu_custom_call" | custom-call | tf_op jit(solution)/shard_map/pallas_call | solution.py:320
  34.4 1.7 %shard_map.47 = f32[1,2,256,1024]{3,2,1,0:T(8,128)} custom-call(bf16[4,1024,128]{2,1,0:T(8,128)(2,1)S(1)} %bitcast.6), custom_call_target="tpu_custom_call" | custom-call | tf_op jit(solution)/shard_map/pallas_call | solution.py:355
